TPU v7x, 256 devices: a whole 4x4x8 slice. The times are simulated.
256 devices in a mesh: dp: 16 (over y, x_hi, core), expert: 16 (over x_lo, z).
Axes of the slice: x: 4 (x_hi: 2, x_lo: 2; x = x_hi * 2 + x_lo), y: 4, z: 8, core: 2. Of those that a mesh axis runs over, the one named last changes fastest.
Arguments:
- tokens: bfloat16 [2048, 3584], P('expert', 'dp'), may hold values from -6 to 6
- routes: int32 [2048, 8], replicated, may hold values from 0 to 47, all different within a row; in each aligned block of 2048 rows (0 to 2047, 2048 to 4095, ...) at most 362 rows name the same one
- combine: float32 [2048, 8], replicated, may hold values from 0.02 to 0.5
- w_gate: bfloat16 [48, 3584, 1280], P('expert', 'dp'), may hold values from -0.09375 to 0.09375
- w_up: bfloat16 [48, 3584, 1280], P('expert', 'dp'), may hold values from -0.09375 to 0.09375
- w_down: bfloat16 [48, 1280, 3584], P('expert', None, 'dp'), may hold values from -0.15625 to 0.15625
- cotangent: bfloat16 [2048, 3584], P('expert', 'dp'), may hold values from -6 to 6
Outputs:
- mixed: bfloat16 [2048, 3584], P('expert', 'dp')
- grad_tokens: bfloat16 [2048, 3584], P('expert', 'dp')
- grad_gate: bfloat16 [48, 3584, 1280], P('expert', 'dp')
- grad_up: bfloat16 [48, 3584, 1280], P('expert', 'dp')
- grad_down: bfloat16 [48, 1280, 3584], P('expert', None, 'dp')
Inputs may be any that keep to these rules, and one draw needn't show every extreme that they name: `routes`: each token names 8 different experts; no expert is named by more than 362 tokens, a bound that some block reaches.
All inputs are finite; a program needn't handle non-finite values.
Results may differ from a plain program's by a relative error of at most 0.03.
Values may be sent and summed in bfloat16 or wider, within the bound.
A program may use at most 128 MiB of HBM per device.

v0:
```python
import jax
import jax.numpy as jnp
from jax import lax
from jax.sharding import PartitionSpec as P


def build_slots(routes, combine, first_id, experts, capacity):
    tok_count = routes.shape[0]
    local_ids = first_id + jnp.arange(experts, dtype=jnp.int32)
    matched = routes[:, :, None] == local_ids[None, None, :]
    routed = jnp.any(matched, axis=1)
    weight = jnp.sum(
        jnp.where(matched, combine[:, :, None], jnp.zeros_like(combine)[:, :, None]), axis=1
    )
    ranked = jnp.cumsum(routed.astype(jnp.int32), axis=0) - 1
    slot_pos = jnp.where(routed, ranked, capacity)
    column = jnp.broadcast_to(jnp.arange(experts, dtype=jnp.int32)[None, :], slot_pos.shape)
    row_ids = jnp.broadcast_to(jnp.arange(tok_count, dtype=jnp.int32)[:, None], slot_pos.shape)
    tok_index = (
        jnp.zeros((experts, capacity + 1), jnp.int32)
        .at[column, slot_pos]
        .set(row_ids)[:, :capacity]
    )
    slot_weight = (
        jnp.zeros((experts, capacity + 1), jnp.float32)
        .at[column, slot_pos]
        .set(weight)[:, :capacity]
    )
    slot_live = (
        jnp.zeros((experts, capacity + 1), jnp.float32)
        .at[column, slot_pos]
        .set(routed.astype(jnp.float32))[:, :capacity]
    )
    return (tok_index, slot_weight, slot_live)


def activate(gate, up):
    sig_gate = jax.nn.sigmoid(gate)
    return (gate * sig_gate * up).astype(jnp.bfloat16)


def derive(back, gate, up):
    sig_gate = jax.nn.sigmoid(gate)
    gate_grad = (back * up * sig_gate * (1.0 + gate * (1.0 - sig_gate))).astype(jnp.bfloat16)
    up_grad = (back * gate * sig_gate).astype(jnp.bfloat16)
    return (gate_grad, up_grad)


def body(tokens, routes, combine, w_gate, w_up, w_down, cotangent):
    experts = w_gate.shape[0]
    tok_count = routes.shape[0]
    experts_all = experts * lax.axis_size("expert")
    capacity = min(tok_count, tok_count * routes.shape[1] * 17 // (16 * experts_all))
    first_id = lax.axis_index("expert") * experts
    tok_index, slot_weight, slot_live = build_slots(routes, combine, first_id, experts, capacity)
    gathered, cot_rows = (
        lax.all_gather(tokens, "expert", axis=0, tiled=True),
        lax.all_gather(cotangent, "expert", axis=0, tiled=True),
    )
    picked = gathered[tok_index] * slot_live[:, :, None].astype(jnp.bfloat16)
    gate_part = jnp.einsum("ecd,edf->ecf", picked, w_gate, preferred_element_type=jnp.float32)
    up_part = jnp.einsum("ecd,edf->ecf", picked, w_up, preferred_element_type=jnp.float32)
    gate_sum, up_sum = (
        lax.psum_scatter(
            gate_part.astype(jnp.bfloat16), "dp", scatter_dimension=2, tiled=True
        ).astype(jnp.float32),
        lax.psum_scatter(
            up_part.astype(jnp.bfloat16), "dp", scatter_dimension=2, tiled=True
        ).astype(jnp.float32),
    )
    hidden = lax.all_gather(activate(gate_sum, up_sum), "dp", axis=2, tiled=True)
    slot_out = jnp.einsum("ecf,efd->ecd", hidden, w_down, preferred_element_type=jnp.float32)
    out_rows = (
        jnp.zeros((tok_count, tokens.shape[1]), jnp.float32)
        .at[tok_index]
        .add(slot_out * slot_weight[:, :, None])
    )
    mixed = lax.psum_scatter(
        out_rows.astype(jnp.bfloat16), "expert", scatter_dimension=0, tiled=True
    )
    cot_slots = (cot_rows[tok_index].astype(jnp.float32) * slot_weight[:, :, None]).astype(
        jnp.bfloat16
    )
    grad_down = jnp.einsum(
        "ecf,ecd->efd", hidden, cot_slots, preferred_element_type=jnp.float32
    ).astype(jnp.bfloat16)
    back_part = jnp.einsum("ecd,efd->ecf", cot_slots, w_down, preferred_element_type=jnp.float32)
    back_share = lax.psum_scatter(
        back_part.astype(jnp.bfloat16), "dp", scatter_dimension=2, tiled=True
    ).astype(jnp.float32)
    gate_share, up_share = derive(back_share, gate_sum, up_sum)
    gate_grad, up_grad = (
        lax.all_gather(gate_share, "dp", axis=2, tiled=True),
        lax.all_gather(up_share, "dp", axis=2, tiled=True),
    )
    grad_gate = jnp.einsum(
        "ecd,ecf->edf", picked, gate_grad, preferred_element_type=jnp.float32
    ).astype(jnp.bfloat16)
    grad_up = jnp.einsum(
        "ecd,ecf->edf", picked, up_grad, preferred_element_type=jnp.float32
    ).astype(jnp.bfloat16)
    input_slot = jnp.einsum("ecf,edf->ecd", gate_grad, w_gate, preferred_element_type=jnp.float32)
    input_slot = input_slot + jnp.einsum(
        "ecf,edf->ecd", up_grad, w_up, preferred_element_type=jnp.float32
    )
    in_rows = jnp.zeros((tok_count, tokens.shape[1]), jnp.float32).at[tok_index].add(input_slot)
    grad_tokens = lax.psum_scatter(
        in_rows.astype(jnp.bfloat16), "expert", scatter_dimension=0, tiled=True
    )
    return (mixed, grad_tokens, grad_gate, grad_up, grad_down)


def solution(mesh):
    in_specs = (
        P("expert", "dp"),
        P(),
        P(),
        P("expert", "dp", None),
        P("expert", "dp", None),
        P("expert", None, "dp"),
        P("expert", "dp"),
    )
    out_specs = (
        P("expert", "dp"),
        P("expert", "dp"),
        P("expert", "dp", None),
        P("expert", "dp", None),
        P("expert", None, "dp"),
    )
    return jax.shard_map(body, mesh=mesh, in_specs=in_specs, out_specs=out_specs, check_vma=False)
```

profile of v0, /device:TPU:2, one launch (start us, length us, event | category | flops | bytes accessed | tf_op | source)
XLA Modules:
  0.0 695.4 jit_solution(15996436086709534855)
XLA Ops:
  7.2 1.1 compare_reduce_fusion
  8.3 1.0 fusion.22
  9.4 0.9 copy.83
  10.3 0.9 reduce-window.6
  13.4 41.5 %all_gather.17 = bf16[2048,224]{1,0:T(8,128)(2,1)S(1)} all-gather(bf16[128,224]{1,0:T(8,128)(2,1)S(1)} %copy.83), channel_id=1, replica_groups=mesh['dp'=16,'expert'=16] {'expert'}, dimensions={0}, use_global_device_ids=true | all-gather | bytes 974848 | tf_op jit(solution)/shard_map/all_gather | solution.py:58
  54.9 1.3 copy.77
  56.2 1.9 reshape.90
  58.1 1.3 copy.81
  59.5 1.9 reshape.104
  61.3 23.0 %scatter_custom_fusion.4 = f32[1089]{0:T(1024)S(1)} fusion(s32[6144]{0:T(1024)S(1)} %reshape.90, f32[6144]{0:T(1024)S(1)} %reshape.104, f32[]{:T(128)} %constant.10.clone.1), kind=kCustom, calls=%fused_computation.61 | custom fusion | bytes 4360
  84.4 1.0 broadcast_in_dim.34
  85.4 1.9 reshape.92
  87.3 23.0 %scatter_custom_fusion.2 = s32[1089]{0:T(1024)S(1)} fusion(s32[6144]{0:T(1024)S(1)} %reshape.90, s32[6144]{0:T(1024)S(1)} %reshape.92, s32[]{:T(128)} %constant.11.clone.1), kind=kCustom, calls=%fused_computation.65 | custom fusion | bytes 4360
  110.5 4.6 gather_fusion.1
  115.1 2.2 reshape.116
  117.4 1.6 copy.84
  119.0 2.9 convolution_convert_fusion
  123.9 23.0 %scatter_custom_fusion.3 = f32[1089]{0:T(1024)S(1)} fusion(s32[6144]{0:T(1024)S(1)} %reshape.90, f32[6144]{0:T(1024)S(1)} %reshape.98, f32[]{:T(128)} %constant.10.clone.1), kind=kCustom, calls=%fused_computation.63 | custom fusion | bytes 4360
  147.0 35.8 %all_gather.15 = bf16[2048,224]{1,0:T(8,128)(2,1)S(1)} all-gather(bf16[128,224]{1,0:T(8,128)(2,1)S(1)} %copy.78), channel_id=1, replica_groups=mesh['dp'=16,'expert'=16] {'expert'}, dimensions={0}, use_global_device_ids=true | all-gather | bytes 974848 | tf_op jit(solution)/shard_map/all_gather | solution.py:57
  182.7 4.6 gather_fusion
  187.4 1.3 reshape.59
  188.9 4.4 convolution_convert_fusion.1
  193.4 4.4 convolution_convert_fusion.2
  197.9 3.5 reduce-scatter.12.cloned.1.call-done
  201.4 85.3 %reduce-scatter.8.cloned.1.call-done = bf16[3,362,80]{1,2,0:T(8,128)(2,1)} async-done(((bf16[3,362,1280]{1,2,0:T(8,128)(2,1)}), bf16[3,362,80]{1,2,0:T(8,128)(2,1)}) %reduce-scatter.8.cloned.1.call-update) | async-done | bytes 173776 | tf_op jit(solution)/shard_map/reduce_scatter | solution.py:67
  286.7 85.3 %reduce-scatter.6.cloned.1.call-done = bf16[3,362,80]{1,2,0:T(8,128)(2,1)} async-done(((bf16[3,362,1280]{1,2,0:T(8,128)(2,1)}), bf16[3,362,80]{1,2,0:T(8,128)(2,1)}) %reduce-scatter.6.cloned.1.call-update) | async-done | bytes 173776 | tf_op jit(solution)/shard_map/reduce_scatter | solution.py:64
  372.0 2.1 fusion.13
  375.4 53.8 %all-gather.4.cloned.1.call-done = bf16[3,362,1280]{1,2,0:T(8,128)(2,1)} async-done(((bf16[3,362,80]{1,2,0:T(8,128)(2,1)}), bf16[3,362,1280]{1,2,0:T(8,128)(2,1)}) %all-gather.4.cloned.1.call-update) | async-done | bytes 2780176 | tf_op jit(solution)/shard_map/all_gather | solution.py:71
  429.1 3.8 convolution_multiply_fusion
  433.0 1.6 copy.82
  434.6 1.1 reshape.78
  435.7 10.0 %scatter_custom_fusion = f32[2048,224]{1,0:T(8,128)} fusion(s32[1086]{0:T(1024)S(1)} %reshape.76, f32[1086,224]{1,0:T(8,128)} %reshape.78, f32[]{:T(128)} %constant.10.clone.1), kind=kCustom, calls=%fused_computation.17 | custom fusion | flops 243264 | bytes 1835520 | tf_op jit(solution)/shard_map/scatter-add | solution.py:76
  445.6 2.7 convert_element_type.65
  448.6 37.8 %all-gather.6.cloned.1.call-done = bf16[3,362,1280]{1,2,0:T(8,128)(2,1)} async-done(((bf16[3,362,80]{1,2,0:T(8,128)(2,1)}), bf16[3,362,1280]{1,2,0:T(8,128)(2,1)}) %all-gather.6.cloned.1.call-update) | async-done | bytes 2780176 | tf_op jit(solution)/shard_map/all_gather | solution.py:93
  486.4 3.4 fusion.32
  489.8 53.9 %all-gather.8.cloned.1.call-done = bf16[3,362,1280]{1,2,0:T(8,128)(2,1)} async-done(((bf16[3,362,80]{1,2,0:T(8,128)(2,1)}), bf16[3,362,1280]{1,2,0:T(8,128)(2,1)}) %all-gather.8.cloned.1.call-update) | async-done | bytes 2780176 | tf_op jit(solution)/shard_map/all_gather | solution.py:94
  543.7 4.4 convolution_add_fusion
  548.1 1.6 copy.85
  549.7 1.1 reshape.86
  550.8 10.0 %scatter_custom_fusion.1 = f32[2048,224]{1,0:T(8,128)} fusion(s32[1086]{0:T(1024)S(1)} %reshape.76, f32[1086,224]{1,0:T(8,128)} %reshape.86, f32[]{:T(128)} %constant.10.clone.1), kind=kCustom, calls=%fused_computation.15 | custom fusion | flops 243264 | bytes 1835520 | tf_op jit(solution)/shard_map/scatter-add | solution.py:106
  560.8 2.7 convert_element_type.72
  563.5 4.3 convolution_convert_fusion.5
  567.8 2.3 convolution_convert_fusion.4
  570.2 2.3 convolution_convert_fusion.3
  572.5 44.1 %reduce-scatter.10.cloned.1.call-done = bf16[128,224]{1,0:T(8,128)(2,1)} async-done(((bf16[2048,224]{1,0:T(8,128)(2,1)}), bf16[128,224]{1,0:T(8,128)(2,1)}) %reduce-scatter.10.cloned.1.call-update) | async-done | bytes 57360 | tf_op jit(solution)/shard_map/reduce_scatter | solution.py:78
  616.6 1.6 copy.86
  618.2 68.8 %reduce-scatter.14.cloned.1.call-done = bf16[128,224]{1,0:T(8,128)(2,1)} async-done(((bf16[2048,224]{1,0:T(8,128)(2,1)}), bf16[128,224]{1,0:T(8,128)(2,1)}) %reduce-scatter.14.cloned.1.call-update) | async-done | bytes 57360 | tf_op jit(solution)/shard_map/reduce_scatter | solution.py:107
  687.0 1.6 copy.87
  (51 shorter events, 6.5 us)
Async XLA Ops:
  7.2 111.8 %copy-start = (bf16[3,1280,224]{1,2,0:T(8,128)(2,1)S(1)}, bf16[3,1280,224]{1,2,0:T(8,128)(2,1)}, u32[]{:S(2)}) copy-start(bf16[3,1280,224]{1,2,0:T(8,128)(2,1)} %param.12) | copy-start | bytes 5160964
  7.2 194.2 %reduce-scatter.12.cloned.1.call-start = ((), (), s32[]{:S(2)}) async-start(), calls=%async_computation.9 | async-start | bytes 3133440 | tf_op jit(solution)/shard_map/reduce_scatter | solution.py:88
  119.0 2.9 copy-start.3
  121.9 0.8 copy-start.5
  121.9 164.8 %reduce-scatter.8.cloned.1.call-start = ((), (), s32[]{:S(2)}) async-start(), calls=%async_computation.6 | async-start | bytes 3133440 | tf_op jit(solution)/shard_map/reduce_scatter | solution.py:67
  193.4 178.6 %reduce-scatter.6.cloned.1.call-start = ((), (), s32[]{:S(2)}) async-start(), calls=%async_computation.5 | async-start | bytes 3133440 | tf_op jit(solution)/shard_map/reduce_scatter | solution.py:64
  197.9 231.3 %all-gather.4.cloned.1.call-start = ((), (), s32[]{:S(2)}) async-start(), calls=%async_computation.7 | async-start | bytes 3133440 | tf_op jit(solution)/shard_map/all_gather | solution.py:71
  374.1 112.3 %all-gather.6.cloned.1.call-start = ((), (), s32[]{:S(2)}) async-start(), calls=%async_computation.10 | async-start | bytes 3133440 | tf_op jit(solution)/shard_map/all_gather | solution.py:93
  374.7 169.0 %all-gather.8.cloned.1.call-start = ((), (), s32[]{:S(2)}) async-start(), calls=%async_computation.11 | async-start | bytes 3133440 | tf_op jit(solution)/shard_map/all_gather | solution.py:94
  375.3 241.3 %reduce-scatter.10.cloned.1.call-start = ((), (), s32[]{:S(2)}) async-start(), calls=%async_computation.8 | async-start | bytes 1114112 | tf_op jit(solution)/shard_map/reduce_scatter | solution.py:78
  448.3 238.7 %reduce-scatter.14.cloned.1.call-start = ((), (), s32[]{:S(2)}) async-start(), calls=%async_computation.12 | async-start | bytes 1114112 | tf_op jit(solution)/shard_map/reduce_scatter | solution.py:107
  563.5 4.3 copy-start.1
  567.8 2.4 copy-start.2
  567.8 2.4 copy-start.4
Sparse Core Ops, SparseCore 0:
  122.0 79.3 reduce-scatter.11
  205.9 80.7 reduce-scatter.7
  291.2 80.8 reduce-scatter.5
  375.1 53.9 all-gather.3
  432.3 54.1 all-gather.5
  489.6 54.1 all-gather.7
  546.2 70.3 reduce-scatter.9
  619.3 67.6 reduce-scatter.13
where the time goes:
time: 697 us; the launch traced here: 695 us
  waiting for transfers between devices  434 us (62%)
  local copies, waits for them, and re-layouts  105 us (15%)
  blocking collectives  77.3 us (11%)
  other arithmetic  32.3 us (5%)
  matrix products  32.3 us (5%)
  between operations  14.3 us (2%)
    reduce_scatter x1, waiting for transfers between devices, body(): lax.psum_scatter(gate_part.astype(jnp.bfloat16), 'dp', scatter_dimension=...  85.3 us
    reduce_scatter x1, waiting for transfers between devices, body(): lax.psum_scatter(up_part.astype(jnp.bfloat16), 'dp', scatter_dimension=2,...  85.3 us
    unnamed x22, local copies, waits for them, and re-layouts  77.1 us
    reduce_scatter x1, waiting for transfers between devices, body(): lax.psum_scatter(in_rows.astype(jnp.bfloat16), 'expert', scatter_dimensio...  68.8 us
    all_gather x1, waiting for transfers between devices, body(): lax.all_gather(up_share, 'dp', axis=2, tiled=True)  53.9 us
    all_gather x1, waiting for transfers between devices, body(): lax.all_gather(activate(gate_sum, up_sum), 'dp', axis=2, tiled=True)  53.8 us
    reduce_scatter x1, waiting for transfers between devices, body(): lax.psum_scatter(out_rows.astype(jnp.bfloat16), 'expert', scatter_dimensi...  44.1 us
    all_gather x1, blocking collectives, body(): lax.all_gather(cotangent, 'expert', axis=0, tiled=True)  41.5 us
  transfers between devices with their start and end apart: 8, of which 8 were waited for; matrix products, arithmetic and copies ran while one was open for 13% of the time, Pallas kernels for 0%

commit v1 on v0

v1 whole, which is shorter than its diff:
```python
import functools

import jax
import jax.numpy as jnp
from jax import lax
from jax.experimental import pallas as pl
from jax.experimental.pallas import tpu as pltpu
from jax.sharding import PartitionSpec as P

MESH = pl.DeviceIdType.MESH
BF = jnp.bfloat16
F32 = jnp.float32

SK = 2
CP = 384
ROWS = 48
WA = 384
WB = 128


def dot(a, b):
    return jnp.dot(a, b, preferred_element_type=F32)


def dot_nt(a, b):
    return lax.dot_general(a, b, (((1,), (1,)), ((), ())), preferred_element_type=F32)


def dot_tn(a, b):
    return lax.dot_general(a, b, (((0,), (0,)), ((), ())), preferred_element_type=F32)


def kernel(
    tok, cot, routes, combine, wg, wu, wd,
    mixed_out, gt_out, gg_out, gu_out, gd_out,
    W, WD, TK, A, WT, PK, PT, PSa, PSb, Qa, Qb, CRa, CRb,
    Y1a, Y2a, Xa, XSa, Xb, Y1b, Y2b, GUa, GUb, Fa, Fb,
    YT, MP, MR, MX, MXS, GGs, GUs, GDs, TP, TPB,
    wsem, osem, rs_s, rs_r, ag_s, ag_r, tk_s, tk_r, m_s, m_r,
):
    experts, width = wg.shape[0], wg.shape[1]
    half = wg.shape[2] // 2
    tokens = routes.shape[1]
    d = lax.axis_index("dp")
    ex = lax.axis_index("expert")
    y, xh, c = d // 4, (d // 2) % 2, d % 2
    xl, z = ex // 8, ex % 8
    yr, yl, yo = (y + 1) % 4, (y + 3) % 4, (y + 2) % 4
    xo, co, xlo = 1 - xh, 1 - c, 1 - xl

    def dev(yy, xx, cc, ll, zz):
        return (yy * 4 + xx * 2 + cc, ll * 8 + zz)

    CORE = dev(y, xh, co, xl, z)
    YR = dev(yr, xh, c, xl, z)
    YL = dev(yl, xh, c, xl, z)
    XH = dev(y, xo, c, xl, z)
    XL = dev(y, xh, c, xlo, z)
    ZR = dev(y, xh, c, xl, (z + 1) % 8)
    ZL = dev(y, xh, c, xl, (z + 7) % 8)

    def remote(src, dst, ss, rr, to):
        return pltpu.make_async_remote_copy(
            src_ref=src, dst_ref=dst, send_sem=ss, recv_sem=rr,
            device_id=to, device_id_type=MESH,
        )

    def weight_copies():
        out = []
        for i, w in enumerate((wg, wu)):
            for h in range(2):
                out.append(pltpu.make_async_copy(
                    w.at[:, :, pl.ds(h * half, half)], W.at[i, h], wsem.at[i * 2 + h]))
        for h in range(2):
            out.append(pltpu.make_async_copy(
                wd.at[:, pl.ds(h * half, half), :], WD.at[h], wsem.at[4 + h]))
        return out

    barrier = pltpu.get_barrier_semaphore()
    for peer in (CORE, YR, YL, XH, XL, ZR, ZL):
        pl.semaphore_signal(barrier, inc=1, device_id=peer, device_id_type=MESH)
    for cp in weight_copies():
        cp.start()

    TPB[...] = jnp.zeros_like(TPB)
    for i, src in enumerate((tok, cot)):
        TPB[:, :width] = src[...].astype(F32)
        TK[i, xl, z] = jnp.transpose(TPB[...])[:width].astype(BF)
    pl.semaphore_wait(barrier, 7)

    def tk_x(i):
        r = TK.at[i, xl, z]
        return remote(r, r, tk_s.at[i, 16], tk_r.at[i, 16], XL)

    def tk_z(i, way, s, b):
        zs = (z + 8 - (s - 1)) % 8 if way == 0 else (z + (s - 1)) % 8
        r = TK.at[i, b, zs]
        n = way * 8 + (s - 1) * 2 + b
        return remote(r, r, tk_s.at[i, n], tk_r.at[i, n], ZR if way == 0 else ZL)

    def tk0(i):
        tk_z(i, 0, 1, xl).start()
        tk_z(i, 1, 1, xl).start()
        tk_x(i).start()

    def tk1(i):
        tk_x(i).wait_recv()
        tk_z(i, 0, 1, xlo).start()
        tk_z(i, 1, 1, xlo).start()

    def tk_hop(i, s):
        if s < 3:
            for b in (xl, xlo):
                for way in (0, 1):
                    tk_z(i, way, s, b).wait_recv()
                    tk_z(i, way, s + 1, b).start()
        elif s == 3:
            for way in (0, 1):
                tk_z(i, way, 3, way).wait_recv()
                tk_z(i, way, 4, way).start()
            for way in (0, 1):
                tk_z(i, way, 3, 1 - way).wait_recv()
        else:
            for way in (0, 1):
                tk_z(i, way, 4, way).wait_recv()

    def tk_drain(i):
        tk_x(i).wait_send()
        for way in (0, 1):
            for s in (1, 2, 3):
                for b in (0, 1):
                    tk_z(i, way, s, b).wait_send()
            tk_z(i, way, 4, way).wait_send()

    def token_rows(i):
        return jnp.concatenate([TK[i, n // 8, n % 8] for n in range(16)], axis=1)

    def m_z(i, way, s):
        zd = (z + 5 - s) % 8 if way == 0 else (z + 3 + s) % 8
        n = way * 4 + s - 1
        to = ZR if way == 0 else ZL
        if s == 1:
            return remote(MP.at[i, way, zd], MR.at[i, way, 0, way], m_s.at[i, n], m_r.at[i, n], to)
        return remote(MP.at[i, :, zd], MR.at[i, way, s - 1], m_s.at[i, n], m_r.at[i, n], to)

    def m_x(i):
        return remote(MXS.at[i], MX.at[i], m_s.at[i, 8], m_r.at[i, 8], XL)

    def m_partial(i):
        for q in range(4):
            acc = dot(YT[i, 0], A[0, :, q * 512:(q + 1) * 512])
            for e in range(1, experts):
                acc = acc + dot(YT[i, e], A[e, :, q * 512:(q + 1) * 512])
            acc = acc.astype(BF)
            for j in range(4):
                n = q * 4 + j
                MP[i, n // 8, n % 8] = acc[:, j * 128:(j + 1) * 128]
        m_z(i, 0, 1).start()
        m_z(i, 1, 1).start()

    def m_step(i, s):
        for way in (0, 1):
            zd = (z + 5 - s) % 8 if way == 0 else (z + 3 + s) % 8
            m_z(i, way, s - 1).wait_recv()
            if s == 2:
                MP[i, way, zd] = (MP[i, way, zd].astype(F32) + MR[i, way, 0, way].astype(F32)).astype(BF)
            else:
                for b in (0, 1):
                    MP[i, b, zd] = (MP[i, b, zd].astype(F32) + MR[i, way, s - 2, b].astype(F32)).astype(BF)
            m_z(i, way, s).start()

    def m_sum(i, b):
        return MP[i, b, z].astype(F32) + MR[i, 0, 3, b].astype(F32) + MR[i, 1, 3, b].astype(F32)

    def m_end(i):
        m_z(i, 0, 4).wait_recv()
        m_z(i, 1, 4).wait_recv()
        MXS[i] = m_sum(i, xlo).astype(BF)
        m_x(i).start()

    def m_final(i, out):
        m_x(i).wait_recv()
        TP[0:width, 0:128] = m_sum(i, xl) + MX[i].astype(F32)
        out[...] = jnp.transpose(TP[0:256, 0:128])[:, :width].astype(BF)

    def m_drain(i):
        for way in (0, 1):
            for s in (1, 2, 3, 4):
                m_z(i, way, s).wait_send()
        m_x(i).wait_send()

    def rs(k, n):
        s, r = rs_s.at[k, n], rs_r.at[k, n]
        if n == 0:
            return remote(PSa.at[k], CRa.at[k], s, r, CORE)
        if n == 1:
            return remote(PSb.at[k], CRb.at[k], s, r, CORE)
        if n == 2:
            return remote(Qa.at[k, yo, 0], Y1a.at[k, 0], s, r, YR)
        if n == 3:
            return remote(Qa.at[k, yo, 1], Y1a.at[k, 1], s, r, YL)
        if n == 4:
            return remote(Qa.at[k, yr], Y2a.at[k, 0], s, r, YR)
        if n == 5:
            return remote(Qa.at[k, yl], Y2a.at[k, 1], s, r, YL)
        if n == 6:
            return remote(XSa.at[k], Xa.at[k], s, r, XH)
        if n == 7:
            return remote(Qb.at[k, :, xo], Xb.at[k], s, r, XH)
        if n == 8:
            return remote(Qb.at[k, yo, xh, 0], Y1b.at[k, 0], s, r, YR)
        if n == 9:
            return remote(Qb.at[k, yo, xh, 1], Y1b.at[k, 1], s, r, YL)
        if n == 10:
            return remote(Qb.at[k, yr, xh], Y2b.at[k, 0], s, r, YR)
        return remote(Qb.at[k, yl, xh], Y2b.at[k, 1], s, r, YL)

    def put(ra, rb, k, v):
        v = v.astype(BF)
        ra[k] = v[:, :WA].reshape(4, 2, ROWS, WA)
        for p in range(2):
            rb[k, :, :, p] = v[:, WA + p * WB:WA + (p + 1) * WB].reshape(4, 2, ROWS, WB)

    def s0(k, part):
        put(PSa, PSb, k, part(co))
        rs(k, 0).start()
        rs(k, 1).start()
        put(Qa, Qb, k, part(c))

    def add(ref, idx, other):
        ref[idx] = (ref[idx].astype(F32) + other.astype(F32)).astype(BF)

    def s1(k):
        rs(k, 0).wait_recv()
        add(Qa, (k, yo), CRa[k, yo])
        rs(k, 2).start()
        rs(k, 3).start()
        rs(k, 1).wait_recv()
        for j in range(4):
            add(Qb, (k, j), CRb[k, j])
        rs(k, 7).start()
        for j in (yr, yl, y):
            add(Qa, (k, j), CRa[k, j])

    def s2(k):
        rs(k, 2).wait_recv()
        add(Qa, (k, yr, 0), Y1a[k, 0])
        rs(k, 4).start()
        rs(k, 3).wait_recv()
        add(Qa, (k, yl, 1), Y1a[k, 1])
        rs(k, 5).start()
        rs(k, 7).wait_recv()
        add(Qb, (k, yo, xh), Xb[k, yo])
        rs(k, 8).start()
        rs(k, 9).start()
        for j in (yr, yl, y):
            add(Qb, (k, j, xh), Xb[k, j])

    def sum_a(k, x):
        return Qa[k, y, x].astype(F32) + Y2a[k, 0, x].astype(F32) + Y2a[k, 1, x].astype(F32)

    def s3(k):
        rs(k, 8).wait_recv()
        add(Qb, (k, yr, xh, 0), Y1b[k, 0])
        rs(k, 10).start()
        rs(k, 9).wait_recv()
        add(Qb, (k, yl, xh, 1), Y1b[k, 1])
        rs(k, 11).start()
        rs(k, 4).wait_recv()
        rs(k, 5).wait_recv()
        XSa[k] = sum_a(k, xo).astype(BF)
        rs(k, 6).start()

    def s4(k):
        rs(k, 6).wait_recv()
        va = sum_a(k, xh) + Xa[k].astype(F32)
        rs(k, 10).wait_recv()
        rs(k, 11).wait_recv()
        vb = Qb[k, y, xh].astype(F32) + Y2b[k, 0].astype(F32) + Y2b[k, 1].astype(F32)
        return va, vb

    def hidden_of(gate, up):
        return (gate * jax.nn.sigmoid(gate) * up).astype(BF)

    def grads_of(back, gate, up):
        sg = jax.nn.sigmoid(gate)
        return (back * up * sg * (1.0 + gate * (1.0 - sg))).astype(BF), (back * gate * sg).astype(BF)

    def ag(g, j, n, m):
        s, r = ag_s.at[g, m], ag_r.at[g, m]
        js = pl.ds(j, n)
        if m == 0:
            ref, to = Fa.at[js, c, y, xh], XH
        elif m in (1, 2):
            ref, to = Fa.at[js, c, y, xh], (YR if m == 1 else YL)
        elif m in (3, 4):
            ref, to = Fa.at[js, c, y, xo], (YR if m == 3 else YL)
        elif m == 5:
            ref, to = Fa.at[js, c, yl, 0], YR
        elif m == 6:
            ref, to = Fa.at[js, c, yr, 1], YL
        elif m in (7, 8):
            ref, to = Fb.at[js, c, y, xh], (YR if m == 7 else YL)
        elif m == 9:
            ref, to = Fb.at[js, c, yl, xh, 0], YR
        elif m == 10:
            ref, to = Fb.at[js, c, yr, xh, 1], YL
        elif m == 11:
            ref, to = Fb.at[js, c, :, xh], XH
        elif m == 12:
            ref, to = Fa.at[js, c], CORE
        else:
            ref, to = Fb.at[js, c], CORE
        return remote(ref, ref, s, r, to)

    def ag_stage(i, g, j, n):
        if i == 0:
            for m in (0, 1, 2, 7, 8):
                ag(g, j, n, m).start()
        if i == 1:
            ag(g, j, n, 0).wait_recv()
            ag(g, j, n, 3).start()
            ag(g, j, n, 4).start()
            ag(g, j, n, 7).wait_recv()
            ag(g, j, n, 9).start()
            ag(g, j, n, 8).wait_recv()
            ag(g, j, n, 10).start()
        if i == 2:
            ag(g, j, n, 1).wait_recv()
            ag(g, j, n, 3).wait_recv()
            ag(g, j, n, 5).start()
            ag(g, j, n, 2).wait_recv()
            ag(g, j, n, 4).wait_recv()
            ag(g, j, n, 6).start()
            ag(g, j, n, 9).wait_recv()
            ag(g, j, n, 10).wait_recv()
            ag(g, j, n, 11).start()
        if i == 3:
            ag(g, j, n, 5).wait_recv()
            ag(g, j, n, 6).wait_recv()
            ag(g, j, n, 12).start()
            ag(g, j, n, 11).wait_recv()
            ag(g, j, n, 13).start()
        if i == 4:
            ag(g, j, n, 12).wait_recv()
            ag(g, j, n, 13).wait_recv()

    def full(j, h):
        return jnp.concatenate(
            [Fa[j, h].reshape(CP, WA), Fb[j, h, :, :, 0].reshape(CP, WB), Fb[j, h, :, :, 1].reshape(CP, WB)], axis=1)

    def out_copy(i, e):
        src, dst = ((GGs, gg_out), (GUs, gu_out), (GDs, gd_out))[i]
        return pltpu.make_async_copy(src.at[e], dst.at[e], osem.at[i, e])

    def turn(v):
        TP[:, :width] = v
        return jnp.transpose(TP[...])[:width].astype(BF)

    def use_hidden(e):
        acc = jnp.zeros((CP, width), F32)
        for h in range(2):
            f = full(e, h)
            acc = acc + dot(f, WD[h, e])
            GDs[e, h * half:(h + 1) * half] = dot_tn(f, PK[1, e]).astype(BF)
        out_copy(2, e).start()
        YT[0, e] = turn(acc * WT[e, :, 0:1])

    def use_grads(e):
        acc = jnp.zeros((CP, width), F32)
        for i, stage in ((0, GGs), (1, GUs)):
            for h in range(2):
                f = full(experts + 2 * e + i, h)
                acc = acc + dot_nt(f, W[i, h, e])
                stage[e, :, h * half:(h + 1) * half] = dot(PT[e], f).astype(BF)
            out_copy(i, e).start()
        YT[1, e] = turn(acc)

    tk0(0)
    TP[...] = jnp.zeros_like(TP)
    lane = lax.broadcasted_iota(jnp.int32, (1, tokens), 1)
    for e in range(experts):
        same = routes[...] == ex * experts + e
        routed = jnp.max(jnp.where(same, 1, 0), axis=0, keepdims=True)
        weight = jnp.sum(jnp.where(same, combine[...], 0.0), axis=0, keepdims=True)
        rank = jnp.broadcast_to(routed, (8, tokens))
        lanes = jnp.broadcast_to(lane, (8, tokens))
        step = 1
        while step < tokens:
            rank = rank + jnp.where(lanes >= step, pltpu.roll(rank, step, 1), 0)
            step *= 2
        pos = jnp.where(routed > 0, rank[0:1] - 1, -1)
        if e == 0:
            tk1(0)

        def fill(i, _, e=e, pos=pos, weight=weight):
            at = pl.ds(pl.multiple_of(i * 32, 32), 32)
            hit = lax.broadcasted_iota(jnp.int32, (32, tokens), 0) + i * 32 == pos
            A[e, at] = jnp.where(hit, 1.0, 0.0).astype(BF)
            WT[e, at] = jnp.broadcast_to(
                jnp.sum(jnp.where(hit, weight, 0.0), axis=1, keepdims=True), (32, 128))
            return 0

        lax.fori_loop(0, CP // 32, fill, 0)
        tk_hop(0, e + 1)
    tk_hop(0, 4)
    for cp in weight_copies():
        cp.wait()
    rows = token_rows(0)
    for e in range(experts):
        v = dot_nt(A[e], rows)
        PK[0, e] = v.astype(BF)
        PT[e] = turn(v)

    gu = 2 * experts
    items = gu + experts
    ag_h = 1 + 4 * SK
    ag_p = gu + 4 * SK
    last = ag_p + experts - 1 + 4 * SK

    def tick(t, _):
        def at(k, lo, hi, f):
            @pl.when(jnp.logical_and(k >= lo, k < hi))
            def _():
                f(k)

        def on(k, f):
            @pl.when(t == k)
            def _():
                f()

        at(t, 0, gu, lambda k: s0(k, lambda h: dot(PK[0, k // 2], W[k % 2, h, k // 2])))
        at(t, gu, items, lambda k: s0(k, lambda h: dot_nt(PK[1, k - gu], WD[h, k - gu])))
        at(t - SK, 0, items, s1)
        at(t - 2 * SK, 0, items, s2)
        at(t - 3 * SK, 0, items, s3)

        def end(k):
            va, vb = s4(k)

            @pl.when(k < gu)
            def _():
                GUa[k % 2, k // 2] = va
                GUb[k % 2, k // 2] = vb

            @pl.when(jnp.logical_and(k < gu, k % 2 == 1))
            def _():
                e = k // 2
                Fa[e, c, y, xh] = hidden_of(GUa[0, e], va)
                Fb[e, c, y, xh] = hidden_of(GUb[0, e], vb)
                ag_stage(0, e, e, 1)

            @pl.when(k >= gu)
            def _():
                e = k - gu
                j = experts + 2 * e
                Fa[j, c, y, xh], Fa[j + 1, c, y, xh] = grads_of(va, GUa[0, e], GUa[1, e])
                Fb[j, c, y, xh], Fb[j + 1, c, y, xh] = grads_of(vb, GUb[0, e], GUb[1, e])
                ag_stage(0, experts + e, j, 2)

        at(t - 4 * SK, 0, items, end)

        for i in range(1, 5):
            u = t - ag_h - i * SK

            @pl.when(jnp.logical_and(jnp.logical_and(u >= 0, u < 2 * experts), u % 2 == 0))
            def _(u=u, i=i):
                e = u // 2
                ag_stage(i, e, e, 1)
                if i == 4:
                    use_hidden(e)

            def grads_stage(e, i=i):
                ag_stage(i, experts + e, experts + 2 * e, 2)
                if i == 4:
                    use_grads(e)

            at(t - ag_p - i * SK, 0, experts, grads_stage)

        on(0, lambda: tk0(1))
        on(1, lambda: tk1(1))
        on(2, lambda: tk_hop(1, 1))
        on(3, lambda: tk_hop(1, 2))
        on(4, lambda: tk_hop(1, 3))

        def cot_slots():
            tk_hop(1, 4)
            crow = token_rows(1)
            for e in range(experts):
                PK[1, e] = (dot_nt(A[e], crow) * WT[e, :, 0:1]).astype(BF)

        on(gu - 1, cot_slots)
        m0 = ag_h + 2 * (experts - 1) + 4 * SK
        on(m0, lambda: m_partial(0))
        on(m0 + 1, lambda: m_step(0, 2))
        on(m0 + 2, lambda: m_step(0, 3))
        return 0

    lax.fori_loop(0, last + 1, tick, 0)

    m_partial(1)
    m_step(0, 4)
    m_step(1, 2)
    m_end(0)
    m_step(1, 3)
    m_final(0, mixed_out)
    m_step(1, 4)
    m_end(1)

    def drain_items(k, _):
        for n in range(12):
            rs(k, n).wait_send()
        return 0

    lax.fori_loop(0, items, drain_items, 0)

    def drain_groups(e, _):
        for m in range(14):
            ag(e, e, 1, m).wait_send()
            ag(experts + e, experts + 2 * e, 2, m).wait_send()
        for i in range(3):
            out_copy(i, e).wait()
        return 0

    lax.fori_loop(0, experts, drain_groups, 0)
    tk_drain(0)
    tk_drain(1)
    m_final(1, gt_out)
    m_drain(0)
    m_drain(1)


def body(tokens, routes, combine, w_gate, w_up, w_down, cotangent):
    experts, width, hidden = w_gate.shape
    half = hidden // 2
    total = routes.shape[0]
    block = tokens.shape[0]
    items = 3 * experts
    vm = pl.BlockSpec(memory_space=pltpu.VMEM)
    hbm = pl.BlockSpec(memory_space=pl.ANY)
    V = pltpu.VMEM
    DMA = pltpu.SemaphoreType.DMA
    scratch = [
        V((2, 2, experts, width, half), BF),
        V((2, experts, half, width), BF),
        V((2, 2, 8, width, block), BF),
        V((experts, CP, total), BF),
        V((experts, CP, 128), F32),
        V((2, experts, CP, width), BF),
        V((experts, width, CP), BF),
        V((items, 4, 2, ROWS, WA), BF),
        V((items, 4, 2, 2, ROWS, WB), BF),
        V((items, 4, 2, ROWS, WA), BF),
        V((items, 4, 2, 2, ROWS, WB), BF),
        V((items, 4, 2, ROWS, WA), BF),
        V((items, 4, 2, 2, ROWS, WB), BF),
        V((items, 2, ROWS, WA), BF),
        V((items, 2, 2, ROWS, WA), BF),
        V((items, ROWS, WA), BF),
        V((items, ROWS, WA), BF),
        V((items, 4, 2, ROWS, WB), BF),
        V((items, 2, ROWS, WB), BF),
        V((items, 2, 2, ROWS, WB), BF),
        V((2, experts, ROWS, WA), F32),
        V((2, experts, 2, ROWS, WB), F32),
        V((items, 2, 4, 2, ROWS, WA), BF),
        V((items, 2, 4, 2, 2, ROWS, WB), BF),
        V((2, experts, width, CP), BF),
        V((2, 2, 8, width, block), BF),
        V((2, 2, 4, 2, width, block), BF),
        V((2, width, block), BF),
        V((2, width, block), BF),
        V((experts, width, hidden), BF),
        V((experts, width, hidden), BF),
        V((experts, hidden, width), BF),
        V((CP, 256), F32),
        V((block, 256), F32),
        DMA((6,)),
        DMA((3, experts)),
        DMA((items, 12)),
        DMA((items, 12)),
        DMA((2 * experts, 14)),
        DMA((2 * experts, 14)),
        DMA((2, 17)),
        DMA((2, 17)),
        DMA((2, 9)),
        DMA((2, 9)),
    ]
    call = pl.pallas_call(
        kernel,
        out_shape=(
            jax.ShapeDtypeStruct(tokens.shape, BF),
            jax.ShapeDtypeStruct(tokens.shape, BF),
            jax.ShapeDtypeStruct(w_gate.shape, BF),
            jax.ShapeDtypeStruct(w_up.shape, BF),
            jax.ShapeDtypeStruct(w_down.shape, BF),
        ),
        in_specs=[vm, vm, vm, vm, hbm, hbm, hbm],
        out_specs=(vm, vm, hbm, hbm, hbm),
        scratch_shapes=scratch,
        compiler_params=pltpu.CompilerParams(
            collective_id=0, has_side_effects=True, vmem_limit_bytes=62 * 2**20
        ),
    )
    return call(tokens, cotangent, routes.T, combine.T, w_gate, w_up, w_down)


def solution(mesh):
    rows = P("expert", "dp")
    wide = P("expert", "dp", None)
    deep = P("expert", None, "dp")
    return jax.shard_map(
        body,
        mesh=mesh,
        in_specs=(rows, P(), P(), wide, wide, deep, rows),
        out_specs=(rows, rows, wide, wide, deep),
        check_vma=False,
    )
```

time: 697 us -> 159 us (0.23)
  waiting for transfers between devices: 434 us -> 0 us
  Pallas kernels: 0 us -> 139 us
  local copies, waits for them, and re-layouts: 105 us -> 17.4 us
  blocking collectives: 77.3 us -> 0 us
  matrix products: 32.3 us -> 0 us
  other arithmetic: 32.3 us -> 0 us
  between operations: 14.3 us -> 0.64 us
    reduce_scatter x5 -> x0, waiting for transfers between devices: 287 us -> none  [the longest x1 85.3 us: body(): lax.psum_scatter(gate_part.astype(jnp.bfloat16), 'dp', scatter_dimension=...]
    all_gather x3 -> x0, waiting for transfers between devices: 146 us -> none  [the longest x1 53.9 us: body(): lax.all_gather(up_share, 'dp', axis=2, tiled=True)]
    pallas_call x0 -> x1, Pallas kernels: none -> 139 us  [body(): return call(tokens, cotangent, routes.T, combine.T, w_gate, w_up, w_down)]
    all_gather x2 -> x0, blocking collectives: 77.3 us -> none  [the longest x1 41.5 us: body(): lax.all_gather(cotangent, 'expert', axis=0, tiled=True)]
    unnamed x22 -> x9, local copies, waits for them, and re-layouts: 77.1 us -> 10.3 us
    dot_general x9 -> x0, matrix products: 32.3 us -> none  [the longest x1 4.42 us: body(): jnp.einsum('ecd,edf->ecf', picked, w_gate, preferred_element_type=jnp.flo...]
    scatter-add x2 -> x0, other arithmetic: 19.9 us -> none  [the longest x1 9.96 us: body(): jnp.zeros((tok_count, tokens.shape[1]), jnp.float32).at[tok_index]]
    gather x4 -> x0, local copies, waits for them, and re-layouts: 10.8 us -> none  [the longest x3 6.2 us: body(): picked = gathered[tok_index] * slot_live[:, :, None].astype(jnp.bfloat16)]
  transfers between devices with their start and end apart: 8 -> 0, of which waited for: 8 -> 0; matrix products, arithmetic and copies ran while one was open for 13% -> 0% of each run, Pallas kernels for 0% -> 0%
where the time goes in v1:
time: 159 us; the launch traced here: 157 us
  Pallas kernels  139 us (87%)
  local copies, waits for them, and re-layouts  17.4 us (11%)
    pallas_call x1, Pallas kernels, body(): return call(tokens, cotangent, routes.T, combine.T, w_gate, w_up, w_down)  139 us
    unnamed x9, local copies, waits for them, and re-layouts  10.3 us
    pallas_call x3, local copies, waits for them, and re-layouts, body(): return call(tokens, cotangent, routes.T, combine.T, w_gate, w_up, w_down)  7.12 us

profile of v1, /device:TPU:2, one launch (start us, length us, event | category | flops | bytes accessed | tf_op | source)
XLA Modules:
  0.0 156.9 jit_solution(4929616803622950699)
XLA Ops:
  0.6 1.6 copy.12.tok
  2.2 1.6 copy.13.cot
  3.7 3.9 %copy.14.wd = bf16[3,1280,224]{2,1,0:T(8,128)(2,1)} copy(bf16[3,1280,224]{1,2,0:T(8,128)(2,1)} %param.12) | data formatting | bytes 3440640 | tf_op args[5]
  7.6 138.9 %shard_map.110 = (bf16[128,224]{1,0:T(8,128)(2,1)}, bf16[128,224]{1,0:T(8,128)(2,1)}, bf16[3,224,1280]{2,1,0:T(8,128)(2,1)}, bf16[3,224,1280]{2,1,0:T(8,128)(2,1)}, bf16[3,1280,224]{2,1,0:T(8,128)(2,1)}) custom-call(bf16[128,224]{1,0:T(8,128)(2,1)} %copy.12.tok, bf16[128,224]{1,0:T(8,128)(2,1)} %copy.13.cot, s32[8,2048]{1,0:T(8,128)} %bitcast.2, ...), custom_call_target="tpu_custom_call" | custom-call | tf_op jit(solution)/shard_map/pallas_call | solution.py:605
  146.5 1.6 copy.15
  148.1 1.6 copy.16
  149.7 0.0 copy-start.1
  149.7 4.0 %copy.17 = bf16[3,1280,224]{1,2,0:T(8,128)(2,1)} copy(bf16[3,1280,224]{2,1,0:T(8,128)(2,1)} %get-tuple-element.9) | data formatting | bytes 3440640 | tf_op jit(solution)/shard_map/pallas_call | solution.py:605
  153.7 0.0 copy-done.1
  153.7 0.0 copy-start
  153.7 1.2 copy.20
  154.9 0.9 copy-done
  155.8 1.2 copy.21
Async XLA Ops:
  149.7 4.0 %copy-start.1 = (bf16[3,224,1280]{2,1,0:T(8,128)(2,1)S(1)}, bf16[3,224,1280]{2,1,0:T(8,128)(2,1)}, u32[]{:S(2)}) copy-start(bf16[3,224,1280]{2,1,0:T(8,128)(2,1)} %get-tuple-element.17) | copy-start | bytes 5160964
  153.7 2.1 %copy-start = (bf16[3,224,1280]{2,1,0:T(8,128)(2,1)S(1)}, bf16[3,224,1280]{2,1,0:T(8,128)(2,1)}, u32[]{:S(2)}) copy-start(bf16[3,224,1280]{2,1,0:T(8,128)(2,1)} %get-tuple-element.18) | copy-start | bytes 5160964

commit v2 on v1

--- a/solution.py
+++ b/solution.py
@@ -1,5 +1,3 @@
-import functools
-
 import jax
 import jax.numpy as jnp
 from jax import lax
@@ -11,7 +9,7 @@
 BF = jnp.bfloat16
 F32 = jnp.float32
 
-SK = 2
+SK = 1
 CP = 384
 ROWS = 48
 WA = 384
@@ -26,16 +24,12 @@
     return lax.dot_general(a, b, (((1,), (1,)), ((), ())), preferred_element_type=F32)
 
 
-def dot_tn(a, b):
-    return lax.dot_general(a, b, (((0,), (0,)), ((), ())), preferred_element_type=F32)
-
-
 def kernel(
     tok, cot, routes, combine, wg, wu, wd,
     mixed_out, gt_out, gg_out, gu_out, gd_out,
-    W, WD, TK, A, WT, PK, PT, PSa, PSb, Qa, Qb, CRa, CRb,
+    W, TK, A, WT, WR, PK, PT, PSa, PSb, Qa, Qb, CRa, CRb,
     Y1a, Y2a, Xa, XSa, Xb, Y1b, Y2b, GUa, GUb, Fa, Fb,
-    YT, MP, MR, MX, MXS, GGs, GUs, GDs, TP, TPB,
+    YT, MP, MR, MX, MXS, GS, TP,
     wsem, osem, rs_s, rs_r, ag_s, ag_r, tk_s, tk_r, m_s, m_r,
 ):
     experts, width = wg.shape[0], wg.shape[1]
@@ -65,15 +59,15 @@
             device_id=to, device_id_type=MESH,
         )
 
+    def sent(ref, sem):
+        remote(ref, ref, sem, sem, CORE).wait_send()
+
     def weight_copies():
         out = []
-        for i, w in enumerate((wg, wu)):
+        for i, w in enumerate((wg, wu, wd)):
             for h in range(2):
                 out.append(pltpu.make_async_copy(
                     w.at[:, :, pl.ds(h * half, half)], W.at[i, h], wsem.at[i * 2 + h]))
-        for h in range(2):
-            out.append(pltpu.make_async_copy(
-                wd.at[:, pl.ds(h * half, half), :], WD.at[h], wsem.at[4 + h]))
         return out
 
     barrier = pltpu.get_barrier_semaphore()
@@ -82,21 +76,19 @@
     for cp in weight_copies():
         cp.start()
 
-    TPB[...] = jnp.zeros_like(TPB)
     for i, src in enumerate((tok, cot)):
-        TPB[:, :width] = src[...].astype(F32)
-        TK[i, xl, z] = jnp.transpose(TPB[...])[:width].astype(BF)
+        TK[i, xl, z] = src[...]
     pl.semaphore_wait(barrier, 7)
 
     def tk_x(i):
         r = TK.at[i, xl, z]
-        return remote(r, r, tk_s.at[i, 16], tk_r.at[i, 16], XL)
+        return remote(r, r, tk_s.at[i, 2], tk_r.at[i, 16], XL)
 
     def tk_z(i, way, s, b):
         zs = (z + 8 - (s - 1)) % 8 if way == 0 else (z + (s - 1)) % 8
         r = TK.at[i, b, zs]
         n = way * 8 + (s - 1) * 2 + b
-        return remote(r, r, tk_s.at[i, n], tk_r.at[i, n], ZR if way == 0 else ZL)
+        return remote(r, r, tk_s.at[i, way], tk_r.at[i, n], ZR if way == 0 else ZL)
 
     def tk0(i):
         tk_z(i, 0, 1, xl).start()
@@ -127,10 +119,7 @@
     def tk_drain(i):
         tk_x(i).wait_send()
         for way in (0, 1):
-            for s in (1, 2, 3):
-                for b in (0, 1):
-                    tk_z(i, way, s, b).wait_send()
-            tk_z(i, way, 4, way).wait_send()
+            sent(TK.at[i, 0, pl.ds(0, 7)], tk_s.at[i, way])
 
     def token_rows(i):
         return jnp.concatenate([TK[i, n // 8, n % 8] for n in range(16)], axis=1)
@@ -140,11 +129,11 @@
         n = way * 4 + s - 1
         to = ZR if way == 0 else ZL
         if s == 1:
-            return remote(MP.at[i, way, zd], MR.at[i, way, 0, way], m_s.at[i, n], m_r.at[i, n], to)
-        return remote(MP.at[i, :, zd], MR.at[i, way, s - 1], m_s.at[i, n], m_r.at[i, n], to)
+            return remote(MP.at[i, way, zd], MR.at[i, way, 0, way], m_s.at[i, way], m_r.at[i, n], to)
+        return remote(MP.at[i, :, zd], MR.at[i, way, s - 1], m_s.at[i, way], m_r.at[i, n], to)
 
     def m_x(i):
-        return remote(MXS.at[i], MX.at[i], m_s.at[i, 8], m_r.at[i, 8], XL)
+        return remote(MXS.at[i], MX.at[i], m_s.at[i, 2], m_r.at[i, 8], XL)
 
     def m_partial(i):
         for q in range(4):
@@ -180,17 +169,15 @@
 
     def m_final(i, out):
         m_x(i).wait_recv()
-        TP[0:width, 0:128] = m_sum(i, xl) + MX[i].astype(F32)
-        out[...] = jnp.transpose(TP[0:256, 0:128])[:, :width].astype(BF)
+        out[...] = (m_sum(i, xl) + MX[i].astype(F32)).astype(BF)
 
     def m_drain(i):
         for way in (0, 1):
-            for s in (1, 2, 3, 4):
-                m_z(i, way, s).wait_send()
+            sent(MP.at[i, 0, pl.ds(0, 7)], m_s.at[i, way])
         m_x(i).wait_send()
 
     def rs(k, n):
-        s, r = rs_s.at[k, n], rs_r.at[k, n]
+        s, r = rs_s.at[n], rs_r.at[k, n]
         if n == 0:
             return remote(PSa.at[k], CRa.at[k], s, r, CORE)
         if n == 1:
@@ -287,7 +274,7 @@
         return (back * up * sg * (1.0 + gate * (1.0 - sg))).astype(BF), (back * gate * sg).astype(BF)
 
     def ag(g, j, n, m):
-        s, r = ag_s.at[g, m], ag_r.at[g, m]
+        s, r = ag_s.at[m], ag_r.at[g, m]
         js = pl.ds(j, n)
         if m == 0:
             ref, to = Fa.at[js, c, y, xh], XH
@@ -350,31 +337,30 @@
             [Fa[j, h].reshape(CP, WA), Fb[j, h, :, :, 0].reshape(CP, WB), Fb[j, h, :, :, 1].reshape(CP, WB)], axis=1)
 
     def out_copy(i, e):
-        src, dst = ((GGs, gg_out), (GUs, gu_out), (GDs, gd_out))[i]
-        return pltpu.make_async_copy(src.at[e], dst.at[e], osem.at[i, e])
+        return pltpu.make_async_copy(GS.at[i, e], (gg_out, gu_out, gd_out)[i].at[e], osem.at[i])
 
     def turn(v):
         TP[:, :width] = v
         return jnp.transpose(TP[...])[:width].astype(BF)
 
     def use_hidden(e):
-        acc = jnp.zeros((CP, width), F32)
+        acc = jnp.zeros((width, CP), F32)
         for h in range(2):
             f = full(e, h)
-            acc = acc + dot(f, WD[h, e])
-            GDs[e, h * half:(h + 1) * half] = dot_tn(f, PK[1, e]).astype(BF)
+            acc = acc + dot_nt(W[2, h, e], f)
+            GS[2, e, :, h * half:(h + 1) * half] = dot(PT[1, e], f).astype(BF)
         out_copy(2, e).start()
-        YT[0, e] = turn(acc * WT[e, :, 0:1])
+        YT[0, e] = (acc * WR[e, 0:1]).astype(BF)
 
     def use_grads(e):
-        acc = jnp.zeros((CP, width), F32)
-        for i, stage in ((0, GGs), (1, GUs)):
+        acc = jnp.zeros((width, CP), F32)
+        for i in range(2):
             for h in range(2):
                 f = full(experts + 2 * e + i, h)
-                acc = acc + dot_nt(f, W[i, h, e])
-                stage[e, :, h * half:(h + 1) * half] = dot(PT[e], f).astype(BF)
+                acc = acc + dot_nt(W[i, h, e], f)
+                GS[i, e, :, h * half:(h + 1) * half] = dot(PT[0, e], f).astype(BF)
             out_copy(i, e).start()
-        YT[1, e] = turn(acc)
+        YT[1, e] = acc.astype(BF)
 
     tk0(0)
     TP[...] = jnp.zeros_like(TP)
@@ -402,6 +388,7 @@
             return 0
 
         lax.fori_loop(0, CP // 32, fill, 0)
+        WR[e] = jnp.transpose(WT[e])
         tk_hop(0, e + 1)
     tk_hop(0, 4)
     for cp in weight_copies():
@@ -410,7 +397,7 @@
     for e in range(experts):
         v = dot_nt(A[e], rows)
         PK[0, e] = v.astype(BF)
-        PT[e] = turn(v)
+        PT[0, e] = turn(v)
 
     gu = 2 * experts
     items = gu + experts
@@ -430,7 +417,7 @@
                 f()
 
         at(t, 0, gu, lambda k: s0(k, lambda h: dot(PK[0, k // 2], W[k % 2, h, k // 2])))
-        at(t, gu, items, lambda k: s0(k, lambda h: dot_nt(PK[1, k - gu], WD[h, k - gu])))
+        at(t, gu, items, lambda k: s0(k, lambda h: dot(PK[1, k - gu], W[2, h, k - gu])))
         at(t - SK, 0, items, s1)
         at(t - 2 * SK, 0, items, s2)
         at(t - 3 * SK, 0, items, s3)
@@ -487,7 +474,9 @@
             tk_hop(1, 4)
             crow = token_rows(1)
             for e in range(experts):
-                PK[1, e] = (dot_nt(A[e], crow) * WT[e, :, 0:1]).astype(BF)
+                v = dot_nt(A[e], crow) * WT[e, :, 0:1]
+                PK[1, e] = v.astype(BF)
+                PT[1, e] = turn(v)
 
         on(gu - 1, cot_slots)
         m0 = ag_h + 2 * (experts - 1) + 4 * SK
@@ -507,27 +496,51 @@
     m_step(1, 4)
     m_end(1)
 
-    def drain_items(k, _):
-        for n in range(12):
-            rs(k, n).wait_send()
-        return 0
-
-    lax.fori_loop(0, items, drain_items, 0)
-
-    def drain_groups(e, _):
-        for m in range(14):
-            ag(e, e, 1, m).wait_send()
-            ag(experts + e, experts + 2 * e, 2, m).wait_send()
-        for i in range(3):
-            out_copy(i, e).wait()
-        return 0
-
-    lax.fori_loop(0, experts, drain_groups, 0)
+    for n, ref in enumerate((
+        PSa, PSb, Y1a.at[:, 0], Y1a.at[:, 1], Y2a.at[:, 0], Y2a.at[:, 1], XSa, Xb,
+        Y1b.at[:, 0], Y1b.at[:, 1], Y2b.at[:, 0], Y2b.at[:, 1],
+    )):
+        sent(ref, rs_s.at[n])
+    for m in range(14):
+        if m < 7:
+            ref = Fa.at[:, c, y, xh]
+        elif m < 9:
+            ref = Fb.at[:, c, y, xh]
+        elif m < 11:
+            ref = Fb.at[:, c, y, xh, 0]
+        elif m == 11:
+            ref = Fb.at[:, c, :, xh]
+        else:
+            ref = (Fa if m == 12 else Fb).at[:, c]
+        sent(ref, ag_s.at[m])
+    for i in range(3):
+        pltpu.make_async_copy(GS.at[i], (gg_out, gu_out, gd_out)[i], osem.at[i]).wait()
     tk_drain(0)
     tk_drain(1)
     m_final(1, gt_out)
     m_drain(0)
     m_drain(1)
+
+
+def copy_out(*refs):
+    small, large, sem = refs[10:]
+    into, out = [], []
+    for i in range(5):
+        src, dst = refs[i], refs[5 + i]
+        if i < 2:
+            into.append(pltpu.make_async_copy(src, small.at[i], sem.at[i, 0, 0]))
+            out.append(pltpu.make_async_copy(small.at[i], dst, sem.at[i, 0, 1]))
+        else:
+            for e in range(src.shape[0]):
+                into.append(pltpu.make_async_copy(src.at[e], large.at[i - 2, e], sem.at[i, e, 0]))
+                out.append(pltpu.make_async_copy(large.at[i - 2, e], dst.at[e], sem.at[i, e, 1]))
+    for cp in into:
+        cp.start()
+    for first, second in zip(into, out):
+        first.wait()
+        second.start()
+    for cp in out:
+        cp.wait()
 
 
 def body(tokens, routes, combine, w_gate, w_up, w_down, cotangent):
@@ -541,13 +554,13 @@
     V = pltpu.VMEM
     DMA = pltpu.SemaphoreType.DMA
     scratch = [
-        V((2, 2, experts, width, half), BF),
-        V((2, experts, half, width), BF),
+        V((3, 2, experts, width, half), BF),
         V((2, 2, 8, width, block), BF),
         V((experts, CP, total), BF),
         V((experts, CP, 128), F32),
+        V((experts, 128, CP), F32),
         V((2, experts, CP, width), BF),
-        V((experts, width, CP), BF),
+        V((2, experts, width, CP), BF),
         V((items, 4, 2, ROWS, WA), BF),
         V((items, 4, 2, 2, ROWS, WB), BF),
         V((items, 4, 2, ROWS, WA), BF),
@@ -570,31 +583,24 @@
         V((2, 2, 4, 2, width, block), BF),
         V((2, width, block), BF),
         V((2, width, block), BF),
-        V((experts, width, hidden), BF),
-        V((experts, width, hidden), BF),
-        V((experts, hidden, width), BF),
+        V((3, experts, width, hidden), BF),
         V((CP, 256), F32),
-        V((block, 256), F32),
         DMA((6,)),
-        DMA((3, experts)),
+        DMA((3,)),
+        DMA((12,)),
         DMA((items, 12)),
-        DMA((items, 12)),
+        DMA((14,)),
         DMA((2 * experts, 14)),
-        DMA((2 * experts, 14)),
+        DMA((2, 3)),
         DMA((2, 17)),
-        DMA((2, 17)),
-        DMA((2, 9)),
+        DMA((2, 3)),
         DMA((2, 9)),
     ]
+    small = jax.ShapeDtypeStruct((width, block), BF)
+    large = jax.ShapeDtypeStruct(w_gate.shape, BF)
     call = pl.pallas_call(
         kernel,
-        out_shape=(
-            jax.ShapeDtypeStruct(tokens.shape, BF),
-            jax.ShapeDtypeStruct(tokens.shape, BF),
-            jax.ShapeDtypeStruct(w_gate.shape, BF),
-            jax.ShapeDtypeStruct(w_up.shape, BF),
-            jax.ShapeDtypeStruct(w_down.shape, BF),
-        ),
+        out_shape=(small, small, large, large, large),
         in_specs=[vm, vm, vm, vm, hbm, hbm, hbm],
         out_specs=(vm, vm, hbm, hbm, hbm),
         scratch_shapes=scratch,
@@ -602,7 +608,21 @@
             collective_id=0, has_side_effects=True, vmem_limit_bytes=62 * 2**20
         ),
     )
-    return call(tokens, cotangent, routes.T, combine.T, w_gate, w_up, w_down)
+    results = call(
+        tokens.T, cotangent.T, routes.T, combine.T, w_gate, w_up, jnp.swapaxes(w_down, 1, 2)
+    )
+    mixed, grad_tokens, grad_gate, grad_up, grad_down = pl.pallas_call(
+        copy_out,
+        out_shape=(small, small, large, large, large),
+        in_specs=[hbm] * 5,
+        out_specs=(hbm,) * 5,
+        scratch_shapes=[
+            V((2, width, block), BF),
+            V((3, experts, width, hidden), BF),
+            DMA((5, experts, 2)),
+        ],
+    )(*results)
+    return mixed.T, grad_tokens.T, grad_gate, grad_up, jnp.swapaxes(grad_down, 1, 2)
 
 
 def solution(mesh):

time: 159 us -> 136 us (0.86); the launches traced: 157 us -> 136 us
  local copies, waits for them, and re-layouts: 17.4 us -> 0 us
  Pallas kernels: 139 us -> 135 us
    unnamed x9 -> x0, local copies, waits for them, and re-layouts: 10.3 us -> none
    pallas_call x3 -> x0, local copies, waits for them, and re-layouts: 7.12 us -> none  [body(): return call(tokens, cotangent, routes.T, combine.T, w_gate, w_up, w_down)]
    pallas_call x1 -> x2, Pallas kernels: 139 us -> 135 us  [the longest x1 131 us: body(): call(tokens.T, cotangent.T, routes.T, combine.T, w_gate, w_up, jnp.swapax...]
where the time goes in v2:
time: 136 us
  Pallas kernels  135 us (99%)
    pallas_call x1, Pallas kernels, body(): call(tokens.T, cotangent.T, routes.T, combine.T, w_gate, w_up, jnp.swapax...  131 us
    pallas_call x1, Pallas kernels, body(): pl.pallas_call(copy_out, out_shape=(small, small, large, large, large), i...  4.88 us

profile of v2, /device:TPU:2, one launch (start us, length us, event | category | flops | bytes accessed | tf_op | source)
XLA Modules:
  0.0 136.0 jit_solution(8032792607260363830)
XLA Ops:
  0.6 130.5 %shard_map.110 = (bf16[224,128]{1,0:T(8,128)(2,1)}, bf16[224,128]{1,0:T(8,128)(2,1)}, bf16[3,224,1280]{2,1,0:T(8,128)(2,1)}, bf16[3,224,1280]{2,1,0:T(8,128)(2,1)}, bf16[3,224,1280]{2,1,0:T(8,128)(2,1)}) custom-call(bf16[224,128]{1,0:T(8,128)(2,1)} %bitcast.11, bf16[224,128]{1,0:T(8,128)(2,1)} %bitcast.12, s32[8,2048]{1,0:T(8,128)} %bitcast.9, ...), custom_call_target="tpu_custom_call" | custom-call | tf_op jit(solution)/shard_map/pallas_call | solution.py:611
  131.1 4.9 %shard_map.111 = (bf16[224,128]{1,0:T(8,128)(2,1)}, bf16[224,128]{1,0:T(8,128)(2,1)}, bf16[3,224,1280]{2,1,0:T(8,128)(2,1)}, bf16[3,224,1280]{2,1,0:T(8,128)(2,1)}, bf16[3,224,1280]{2,1,0:T(8,128)(2,1)}) custom-call(bf16[224,128]{1,0:T(8,128)(2,1)} %get-tuple-element.15.refs_0_, bf16[224,128]{1,0:T(8,128)(2,1)} %get-tuple-element.16.refs_1_, ...), custom_call_target="tpu_custom_call" | custom-call | tf_op jit(solution)/shard_map/pallas_call | solution.py:614

commit v3 on v2

--- a/solution.py
+++ b/solution.py
@@ -9,7 +9,8 @@
 BF = jnp.bfloat16
 F32 = jnp.float32
 
-SK = 1
+SUM_AT = (0, 1, 2, 3, 4)
+GATHER_AT = (0, 1, 2, 3, 4)
 CP = 384
 ROWS = 48
 WA = 384
@@ -26,11 +27,11 @@
 
 def kernel(
     tok, cot, routes, combine, wg, wu, wd,
-    mixed_out, gt_out, gg_out, gu_out, gd_out,
+    mixed_out, gt_out, GS,
     W, TK, A, WT, WR, PK, PT, PSa, PSb, Qa, Qb, CRa, CRb,
     Y1a, Y2a, Xa, XSa, Xb, Y1b, Y2b, GUa, GUb, Fa, Fb,
-    YT, MP, MR, MX, MXS, GS, TP,
-    wsem, osem, rs_s, rs_r, ag_s, ag_r, tk_s, tk_r, m_s, m_r,
+    YT, MP, MR, MX, MXS, TP,
+    wsem, rs_s, rs_r, ag_s, ag_r, tk_s, tk_r, m_s, m_r,
 ):
     experts, width = wg.shape[0], wg.shape[1]
     half = wg.shape[2] // 2
@@ -77,104 +78,120 @@
         cp.start()
 
     for i, src in enumerate((tok, cot)):
-        TK[i, xl, z] = src[...]
+        for f in range(2):
+            TK[i, xl, z, f] = src[f * (width // 2):(f + 1) * (width // 2)]
     pl.semaphore_wait(barrier, 7)
 
-    def tk_x(i):
-        r = TK.at[i, xl, z]
-        return remote(r, r, tk_s.at[i, 2], tk_r.at[i, 16], XL)
-
-    def tk_z(i, way, s, b):
+    def tk_x(i, f):
+        r = TK.at[i, xl, z, f]
+        return remote(r, r, tk_s.at[i, 2], tk_r.at[i, 32 + f], XL)
+
+    def tk_z(i, way, s, b, f):
         zs = (z + 8 - (s - 1)) % 8 if way == 0 else (z + (s - 1)) % 8
-        r = TK.at[i, b, zs]
-        n = way * 8 + (s - 1) * 2 + b
+        r = TK.at[i, b, zs, f]
+        n = ((way * 4 + s - 1) * 2 + b) * 2 + f
         return remote(r, r, tk_s.at[i, way], tk_r.at[i, n], ZR if way == 0 else ZL)
 
     def tk0(i):
-        tk_z(i, 0, 1, xl).start()
-        tk_z(i, 1, 1, xl).start()
-        tk_x(i).start()
+        for f in range(2):
+            for way in (0, 1):
+                tk_z(i, way, 1, xl, f).start()
+            tk_x(i, f).start()
 
     def tk1(i):
-        tk_x(i).wait_recv()
-        tk_z(i, 0, 1, xlo).start()
-        tk_z(i, 1, 1, xlo).start()
+        for f in range(2):
+            tk_x(i, f).wait_recv()
+            for way in (0, 1):
+                tk_z(i, way, 1, xlo, f).start()
 
     def tk_hop(i, s):
         if s < 3:
             for b in (xl, xlo):
+                for f in range(2):
+                    for way in (0, 1):
+                        tk_z(i, way, s, b, f).wait_recv()
+                        tk_z(i, way, s + 1, b, f).start()
+        elif s == 3:
+            for f in range(2):
                 for way in (0, 1):
-                    tk_z(i, way, s, b).wait_recv()
-                    tk_z(i, way, s + 1, b).start()
-        elif s == 3:
-            for way in (0, 1):
-                tk_z(i, way, 3, way).wait_recv()
-                tk_z(i, way, 4, way).start()
-            for way in (0, 1):
-                tk_z(i, way, 3, 1 - way).wait_recv()
+                    tk_z(i, way, 3, way, f).wait_recv()
+                    tk_z(i, way, 4, way, f).start()
+            for f in range(2):
+                for way in (0, 1):
+                    tk_z(i, way, 3, 1 - way, f).wait_recv()
         else:
-            for way in (0, 1):
-                tk_z(i, way, 4, way).wait_recv()
+            for f in range(2):
+                for way in (0, 1):
+                    tk_z(i, way, 4, way, f).wait_recv()
 
     def tk_drain(i):
-        tk_x(i).wait_send()
+        sent(TK.at[i, 0, 0], tk_s.at[i, 2])
         for way in (0, 1):
             sent(TK.at[i, 0, pl.ds(0, 7)], tk_s.at[i, way])
 
     def token_rows(i):
-        return jnp.concatenate([TK[i, n // 8, n % 8] for n in range(16)], axis=1)
-
-    def m_z(i, way, s):
-        zd = (z + 5 - s) % 8 if way == 0 else (z + 3 + s) % 8
-        n = way * 4 + s - 1
-        to = ZR if way == 0 else ZL
-        if s == 1:
-            return remote(MP.at[i, way, zd], MR.at[i, way, 0, way], m_s.at[i, way], m_r.at[i, n], to)
-        return remote(MP.at[i, :, zd], MR.at[i, way, s - 1], m_s.at[i, way], m_r.at[i, n], to)
-
-    def m_x(i):
-        return remote(MXS.at[i], MX.at[i], m_s.at[i, 2], m_r.at[i, 8], XL)
+        return jnp.concatenate([TK[i, n // 8, n % 8].reshape(width, 128) for n in range(16)], axis=1)
+
+    def m_dest(way, s):
+        return (z + 5 - s) % 8 if way == 0 else (z + 3 + s) % 8
+
+    def m_z(i, way, s, b, f):
+        n = ((way * 4 + s - 1) * 2 + b) * 2 + f
+        return remote(
+            MP.at[i, b, m_dest(way, s), f], MR.at[i, way, s - 1, b, f],
+            m_s.at[i, way], m_r.at[i, n], ZR if way == 0 else ZL)
+
+    def m_x(i, f):
+        return remote(MXS.at[i, f], MX.at[i, f], m_s.at[i, 2], m_r.at[i, 32 + f], XL)
 
     def m_partial(i):
-        for q in range(4):
+        for q in (2, 0, 3, 1):
             acc = dot(YT[i, 0], A[0, :, q * 512:(q + 1) * 512])
             for e in range(1, experts):
                 acc = acc + dot(YT[i, e], A[e, :, q * 512:(q + 1) * 512])
             acc = acc.astype(BF)
             for j in range(4):
                 n = q * 4 + j
-                MP[i, n // 8, n % 8] = acc[:, j * 128:(j + 1) * 128]
-        m_z(i, 0, 1).start()
-        m_z(i, 1, 1).start()
+                MP[i, n // 8, n % 8] = acc[:, j * 128:(j + 1) * 128].reshape(2, width // 2, 128)
+        for f in range(2):
+            for way in (0, 1):
+                m_z(i, way, 1, way, f).start()
+        for f in range(2):
+            for way in (0, 1):
+                m_z(i, way, 2, 1 - way, f).start()
+
+    def m_add(i, way, s, b, f):
+        m_z(i, way, s - 1, b, f).wait_recv()
+        zd = m_dest(way, s)
+        MP[i, b, zd, f] = (MP[i, b, zd, f].astype(F32) + MR[i, way, s - 2, b, f].astype(F32)).astype(BF)
+        m_z(i, way, s, b, f).start()
 
     def m_step(i, s):
-        for way in (0, 1):
-            zd = (z + 5 - s) % 8 if way == 0 else (z + 3 + s) % 8
-            m_z(i, way, s - 1).wait_recv()
-            if s == 2:
-                MP[i, way, zd] = (MP[i, way, zd].astype(F32) + MR[i, way, 0, way].astype(F32)).astype(BF)
-            else:
-                for b in (0, 1):
-                    MP[i, b, zd] = (MP[i, b, zd].astype(F32) + MR[i, way, s - 2, b].astype(F32)).astype(BF)
-            m_z(i, way, s).start()
-
-    def m_sum(i, b):
-        return MP[i, b, z].astype(F32) + MR[i, 0, 3, b].astype(F32) + MR[i, 1, 3, b].astype(F32)
+        for n in range(1 if s == 2 else 2):
+            for f in range(2):
+                for way in (0, 1):
+                    m_add(i, way, s, way if n == 0 else 1 - way, f)
+
+    def m_sum(i, b, f):
+        m_z(i, 0, 4, b, f).wait_recv()
+        m_z(i, 1, 4, b, f).wait_recv()
+        return MP[i, b, z, f].astype(F32) + MR[i, 0, 3, b, f].astype(F32) + MR[i, 1, 3, b, f].astype(F32)
 
     def m_end(i):
-        m_z(i, 0, 4).wait_recv()
-        m_z(i, 1, 4).wait_recv()
-        MXS[i] = m_sum(i, xlo).astype(BF)
-        m_x(i).start()
+        for f in range(2):
+            MXS[i, f] = m_sum(i, xlo, f).astype(BF)
+            m_x(i, f).start()
 
     def m_final(i, out):
-        m_x(i).wait_recv()
-        out[...] = (m_sum(i, xl) + MX[i].astype(F32)).astype(BF)
+        for f in range(2):
+            own = m_sum(i, xl, f)
+            m_x(i, f).wait_recv()
+            out[f * (width // 2):(f + 1) * (width // 2)] = (own + MX[i, f].astype(F32)).astype(BF)
 
     def m_drain(i):
         for way in (0, 1):
             sent(MP.at[i, 0, pl.ds(0, 7)], m_s.at[i, way])
-        m_x(i).wait_send()
+        sent(MXS.at[i], m_s.at[i, 2])
 
     def rs(k, n):
         s, r = rs_s.at[n], rs_r.at[k, n]
@@ -336,9 +353,6 @@
         return jnp.concatenate(
             [Fa[j, h].reshape(CP, WA), Fb[j, h, :, :, 0].reshape(CP, WB), Fb[j, h, :, :, 1].reshape(CP, WB)], axis=1)
 
-    def out_copy(i, e):
-        return pltpu.make_async_copy(GS.at[i, e], (gg_out, gu_out, gd_out)[i].at[e], osem.at[i])
-
     def turn(v):
         TP[:, :width] = v
         return jnp.transpose(TP[...])[:width].astype(BF)
@@ -349,7 +363,6 @@
             f = full(e, h)
             acc = acc + dot_nt(W[2, h, e], f)
             GS[2, e, :, h * half:(h + 1) * half] = dot(PT[1, e], f).astype(BF)
-        out_copy(2, e).start()
         YT[0, e] = (acc * WR[e, 0:1]).astype(BF)
 
     def use_grads(e):
@@ -359,7 +372,6 @@
                 f = full(experts + 2 * e + i, h)
                 acc = acc + dot_nt(W[i, h, e], f)
                 GS[i, e, :, h * half:(h + 1) * half] = dot(PT[0, e], f).astype(BF)
-            out_copy(i, e).start()
         YT[1, e] = acc.astype(BF)
 
     tk0(0)
@@ -401,9 +413,9 @@
 
     gu = 2 * experts
     items = gu + experts
-    ag_h = 1 + 4 * SK
-    ag_p = gu + 4 * SK
-    last = ag_p + experts - 1 + 4 * SK
+    ag_h = 1 + SUM_AT[4]
+    ag_p = gu + SUM_AT[4]
+    last = ag_p + experts - 1 + GATHER_AT[4]
 
     def tick(t, _):
         def at(k, lo, hi, f):
@@ -418,9 +430,9 @@
 
         at(t, 0, gu, lambda k: s0(k, lambda h: dot(PK[0, k // 2], W[k % 2, h, k // 2])))
         at(t, gu, items, lambda k: s0(k, lambda h: dot(PK[1, k - gu], W[2, h, k - gu])))
-        at(t - SK, 0, items, s1)
-        at(t - 2 * SK, 0, items, s2)
-        at(t - 3 * SK, 0, items, s3)
+        at(t - SUM_AT[1], 0, items, s1)
+        at(t - SUM_AT[2], 0, items, s2)
+        at(t - SUM_AT[3], 0, items, s3)
 
         def end(k):
             va, vb = s4(k)
@@ -445,10 +457,10 @@
                 Fb[j, c, y, xh], Fb[j + 1, c, y, xh] = grads_of(vb, GUb[0, e], GUb[1, e])
                 ag_stage(0, experts + e, j, 2)
 
-        at(t - 4 * SK, 0, items, end)
+        at(t - SUM_AT[4], 0, items, end)
 
         for i in range(1, 5):
-            u = t - ag_h - i * SK
+            u = t - ag_h - GATHER_AT[i]
 
             @pl.when(jnp.logical_and(jnp.logical_and(u >= 0, u < 2 * experts), u % 2 == 0))
             def _(u=u, i=i):
@@ -462,7 +474,7 @@
                 if i == 4:
                     use_grads(e)
 
-            at(t - ag_p - i * SK, 0, experts, grads_stage)
+            at(t - ag_p - GATHER_AT[i], 0, experts, grads_stage)
 
         on(0, lambda: tk0(1))
         on(1, lambda: tk1(1))
@@ -479,7 +491,7 @@
                 PT[1, e] = turn(v)
 
         on(gu - 1, cot_slots)
-        m0 = ag_h + 2 * (experts - 1) + 4 * SK
+        m0 = ag_h + 2 * (experts - 1) + GATHER_AT[4]
         on(m0, lambda: m_partial(0))
         on(m0 + 1, lambda: m_step(0, 2))
         on(m0 + 2, lambda: m_step(0, 3))
@@ -513,8 +525,6 @@
         else:
             ref = (Fa if m == 12 else Fb).at[:, c]
         sent(ref, ag_s.at[m])
-    for i in range(3):
-        pltpu.make_async_copy(GS.at[i], (gg_out, gu_out, gd_out)[i], osem.at[i]).wait()
     tk_drain(0)
     tk_drain(1)
     m_final(1, gt_out)
@@ -522,24 +532,19 @@
     m_drain(1)
 
 
-def copy_out(*refs):
-    small, large, sem = refs[10:]
-    into, out = [], []
-    for i in range(5):
-        src, dst = refs[i], refs[5 + i]
-        if i < 2:
-            into.append(pltpu.make_async_copy(src, small.at[i], sem.at[i, 0, 0]))
-            out.append(pltpu.make_async_copy(small.at[i], dst, sem.at[i, 0, 1]))
-        else:
-            for e in range(src.shape[0]):
-                into.append(pltpu.make_async_copy(src.at[e], large.at[i - 2, e], sem.at[i, e, 0]))
-                out.append(pltpu.make_async_copy(large.at[i - 2, e], dst.at[e], sem.at[i, e, 1]))
-    for cp in into:
+def copy_out(mixed, grad_tokens, grads, mixed_out, gt_out, gg_out, gu_out, gd_out, sem):
+    copies = [
+        pltpu.make_async_copy(mixed, mixed_out, sem.at[0]),
+        pltpu.make_async_copy(grad_tokens, gt_out, sem.at[1]),
+    ]
+    for i, out in enumerate((gg_out, gu_out, gd_out)):
+        for e in range(out.shape[0]):
+            for h in range(2):
+                rows = pl.ds(h * (out.shape[1] // 2), out.shape[1] // 2)
+                copies.append(pltpu.make_async_copy(grads.at[i, e, rows], out.at[e, rows], sem.at[len(copies)]))
+    for cp in copies:
         cp.start()
-    for first, second in zip(into, out):
-        first.wait()
-        second.start()
-    for cp in out:
+    for cp in copies:
         cp.wait()
 
 
@@ -555,7 +560,7 @@
     DMA = pltpu.SemaphoreType.DMA
     scratch = [
         V((3, 2, experts, width, half), BF),
-        V((2, 2, 8, width, block), BF),
+        V((2, 2, 8, 2, width // 2, block), BF),
         V((experts, CP, total), BF),
         V((experts, CP, 128), F32),
         V((experts, 128, CP), F32),
@@ -579,33 +584,31 @@
         V((items, 2, 4, 2, ROWS, WA), BF),
         V((items, 2, 4, 2, 2, ROWS, WB), BF),
         V((2, experts, width, CP), BF),
-        V((2, 2, 8, width, block), BF),
-        V((2, 2, 4, 2, width, block), BF),
-        V((2, width, block), BF),
-        V((2, width, block), BF),
-        V((3, experts, width, hidden), BF),
+        V((2, 2, 8, 2, width // 2, block), BF),
+        V((2, 2, 4, 2, 2, width // 2, block), BF),
+        V((2, 2, width // 2, block), BF),
+        V((2, 2, width // 2, block), BF),
         V((CP, 256), F32),
         DMA((6,)),
-        DMA((3,)),
         DMA((12,)),
         DMA((items, 12)),
         DMA((14,)),
         DMA((2 * experts, 14)),
         DMA((2, 3)),
-        DMA((2, 17)),
+        DMA((2, 34)),
         DMA((2, 3)),
-        DMA((2, 9)),
+        DMA((2, 34)),
     ]
     small = jax.ShapeDtypeStruct((width, block), BF)
     large = jax.ShapeDtypeStruct(w_gate.shape, BF)
     call = pl.pallas_call(
         kernel,
-        out_shape=(small, small, large, large, large),
+        out_shape=(V((width, block), BF), V((width, block), BF), V((3, experts, width, hidden), BF)),
         in_specs=[vm, vm, vm, vm, hbm, hbm, hbm],
-        out_specs=(vm, vm, hbm, hbm, hbm),
+        out_specs=(vm, vm, vm),
         scratch_shapes=scratch,
         compiler_params=pltpu.CompilerParams(
-            collective_id=0, has_side_effects=True, vmem_limit_bytes=62 * 2**20
+            collective_id=0, has_side_effects=True, vmem_limit_bytes=55 * 2**20
         ),
     )
     results = call(
@@ -614,14 +617,11 @@
     mixed, grad_tokens, grad_gate, grad_up, grad_down = pl.pallas_call(
         copy_out,
         out_shape=(small, small, large, large, large),
-        in_specs=[hbm] * 5,
+        in_specs=[vm] * 3,
         out_specs=(hbm,) * 5,
-        scratch_shapes=[
-            V((2, width, block), BF),
-            V((3, experts, width, hidden), BF),
-            DMA((5, experts, 2)),
-        ],
-    )(*results)
+        scratch_shapes=[DMA((2 + 6 * experts,))],
+        compiler_params=pltpu.CompilerParams(vmem_limit_bytes=2**20),
+    )(*(pltpu.with_memory_space_constraint(r, pltpu.VMEM) for r in results))
     return mixed.T, grad_tokens.T, grad_gate, grad_up, jnp.swapaxes(grad_down, 1, 2)
 
 

time: 136 us -> 130 us (0.956)
  Pallas kernels: 135 us -> 129 us
    pallas_call x1, Pallas kernels: 131 us -> 126 us  [body(): call(tokens.T, cotangent.T, routes.T, combine.T, w_gate, w_up, jnp.swapax...]
    pallas_call x1, Pallas kernels: 4.88 us -> 2.51 us  [body(): pl.pallas_call(copy_out, out_shape=(small, small, large, large, large), i...]
where the time goes in v3:
time: 130 us; the launch traced here: 129 us
  Pallas kernels  129 us (99%)
    pallas_call x1, Pallas kernels, body(): call(tokens.T, cotangent.T, routes.T, combine.T, w_gate, w_up, jnp.swapax...  126 us

profile of v3, /device:TPU:2, one launch (start us, length us, event | category | flops | bytes accessed | tf_op | source)
XLA Modules:
  0.0 129.5 jit_solution(5410084384175560576)
XLA Ops:
  0.6 126.3 %shard_map.110 = (bf16[224,128]{1,0:T(8,128)(2,1)S(1)}, bf16[224,128]{1,0:T(8,128)(2,1)S(1)}, bf16[3,3,224,1280]{3,2,1,0:T(8,128)(2,1)S(1)}) custom-call(bf16[224,128]{1,0:T(8,128)(2,1)} %bitcast.11, bf16[224,128]{1,0:T(8,128)(2,1)} %bitcast.12, s32[8,2048]{1,0:T(8,128)} %bitcast.9, f32[8,2048]{1,0:T(8,128)} %bitcast.10, bf16[3,224,1280]{2,1,0:T(8,128)(2,1)} %wg.1, ...), custom_call_target="tpu_custom_call" | custom-call | tf_op jit(solution)/shard_map/pallas_call | solution.py:614
  127.0 2.5 %shard_map.111 = (bf16[224,128]{1,0:T(8,128)(2,1)}, bf16[224,128]{1,0:T(8,128)(2,1)}, bf16[3,224,1280]{2,1,0:T(8,128)(2,1)}, bf16[3,224,1280]{2,1,0:T(8,128)(2,1)}, bf16[3,224,1280]{2,1,0:T(8,128)(2,1)}) custom-call(bf16[224,128]{1,0:T(8,128)(2,1)S(1)} %get-tuple-element.13.mixed, bf16[224,128]{1,0:T(8,128)(2,1)S(1)} %get-tuple-element.14.grad_tokens, ...), custom_call_target="tpu_custom_call" | custom-call | tf_op jit(solution)/shard_map/pallas_call | solution.py:617

commit v4 on v3

--- a/solution.py
+++ b/solution.py
@@ -59,6 +59,9 @@
             src_ref=src, dst_ref=dst, send_sem=ss, recv_sem=rr,
             device_id=to, device_id_type=MESH,
         )
+
+    def came(ref, sem):
+        remote(ref, ref, sem, sem, CORE).wait_recv()
 
     def sent(ref, sem):
         remote(ref, ref, sem, sem, CORE).wait_send()
@@ -194,7 +197,7 @@
         sent(MXS.at[i], m_s.at[i, 2])
 
     def rs(k, n):
-        s, r = rs_s.at[n], rs_r.at[k, n]
+        s, r = rs_s.at[n], rs_r.at[k, {5: 4, 11: 10}.get(n, n)]
         if n == 0:
             return remote(PSa.at[k], CRa.at[k], s, r, CORE)
         if n == 1:
@@ -270,16 +273,14 @@
         rs(k, 9).wait_recv()
         add(Qb, (k, yl, xh, 1), Y1b[k, 1])
         rs(k, 11).start()
-        rs(k, 4).wait_recv()
-        rs(k, 5).wait_recv()
+        came(Y2a.at[k], rs_r.at[k, 4])
         XSa[k] = sum_a(k, xo).astype(BF)
         rs(k, 6).start()
 
     def s4(k):
         rs(k, 6).wait_recv()
         va = sum_a(k, xh) + Xa[k].astype(F32)
-        rs(k, 10).wait_recv()
-        rs(k, 11).wait_recv()
+        came(Y2b.at[k], rs_r.at[k, 10])
         vb = Qb[k, y, xh].astype(F32) + Y2b[k, 0].astype(F32) + Y2b[k, 1].astype(F32)
         return va, vb
 
@@ -291,7 +292,7 @@
         return (back * up * sg * (1.0 + gate * (1.0 - sg))).astype(BF), (back * gate * sg).astype(BF)
 
     def ag(g, j, n, m):
-        s, r = ag_s.at[m], ag_r.at[g, m]
+        s, r = ag_s.at[m], ag_r.at[g, (0, 1, 1, 1, 1, 2, 2, 3, 3, 4, 4, 5, 6, 7)[m]]
         js = pl.ds(j, n)
         if m == 0:
             ref, to = Fa.at[js, c, y, xh], XH
@@ -318,6 +319,7 @@
         return remote(ref, ref, s, r, to)
 
     def ag_stage(i, g, j, n):
+        js = pl.ds(j, n)
         if i == 0:
             for m in (0, 1, 2, 7, 8):
                 ag(g, j, n, m).start()
@@ -325,23 +327,17 @@
             ag(g, j, n, 0).wait_recv()
             ag(g, j, n, 3).start()
             ag(g, j, n, 4).start()
-            ag(g, j, n, 7).wait_recv()
+            came(Fb.at[js, c, 0], ag_r.at[g, 3])
             ag(g, j, n, 9).start()
-            ag(g, j, n, 8).wait_recv()
             ag(g, j, n, 10).start()
         if i == 2:
-            ag(g, j, n, 1).wait_recv()
-            ag(g, j, n, 3).wait_recv()
+            came(Fa.at[js, c, pl.ds(0, 2)], ag_r.at[g, 1])
             ag(g, j, n, 5).start()
-            ag(g, j, n, 2).wait_recv()
-            ag(g, j, n, 4).wait_recv()
             ag(g, j, n, 6).start()
-            ag(g, j, n, 9).wait_recv()
-            ag(g, j, n, 10).wait_recv()
+            came(Fb.at[js, c, 0, 0], ag_r.at[g, 4])
             ag(g, j, n, 11).start()
         if i == 3:
-            ag(g, j, n, 5).wait_recv()
-            ag(g, j, n, 6).wait_recv()
+            came(Fa.at[js, c, 0], ag_r.at[g, 2])
             ag(g, j, n, 12).start()
             ag(g, j, n, 11).wait_recv()
             ag(g, j, n, 13).start()
@@ -369,10 +365,14 @@
         acc = jnp.zeros((width, CP), F32)
         for i in range(2):
             for h in range(2):
+                acc = acc + dot_nt(W[i, h, e], full(experts + 2 * e + i, h))
+        YT[1, e] = acc.astype(BF)
+
+    def weight_grads(e):
+        for i in range(2):
+            for h in range(2):
                 f = full(experts + 2 * e + i, h)
-                acc = acc + dot_nt(W[i, h, e], f)
                 GS[i, e, :, h * half:(h + 1) * half] = dot(PT[0, e], f).astype(BF)
-        YT[1, e] = acc.astype(BF)
 
     tk0(0)
     TP[...] = jnp.zeros_like(TP)
@@ -405,11 +405,13 @@
     tk_hop(0, 4)
     for cp in weight_copies():
         cp.wait()
-    rows = token_rows(0)
-    for e in range(experts):
-        v = dot_nt(A[e], rows)
+
+    def pick(e):
+        v = dot_nt(A[e], token_rows(0))
         PK[0, e] = v.astype(BF)
         PT[0, e] = turn(v)
+
+    pick(0)
 
     gu = 2 * experts
     items = gu + experts
@@ -455,7 +457,8 @@
                 j = experts + 2 * e
                 Fa[j, c, y, xh], Fa[j + 1, c, y, xh] = grads_of(va, GUa[0, e], GUa[1, e])
                 Fb[j, c, y, xh], Fb[j + 1, c, y, xh] = grads_of(vb, GUb[0, e], GUb[1, e])
-                ag_stage(0, experts + e, j, 2)
+                ag_stage(0, j, j, 1)
+                ag_stage(0, j + 1, j + 1, 1)
 
         at(t - SUM_AT[4], 0, items, end)
 
@@ -470,12 +473,19 @@
                     use_hidden(e)
 
             def grads_stage(e, i=i):
-                ag_stage(i, experts + e, experts + 2 * e, 2)
+                ag_stage(i, experts + 2 * e, experts + 2 * e, 1)
+                ag_stage(i, experts + 2 * e + 1, experts + 2 * e + 1, 1)
                 if i == 4:
                     use_grads(e)
 
+                    @pl.when(e < experts - 1)
+                    def _():
+                        weight_grads(e)
+
             at(t - ag_p - GATHER_AT[i], 0, experts, grads_stage)
 
+        for e in range(1, experts):
+            on(e - 1, lambda e=e: pick(e))
         on(0, lambda: tk0(1))
         on(1, lambda: tk1(1))
         on(2, lambda: tk_hop(1, 1))
@@ -500,6 +510,7 @@
     lax.fori_loop(0, last + 1, tick, 0)
 
     m_partial(1)
+    weight_grads(experts - 1)
     m_step(0, 4)
     m_step(1, 2)
     m_end(0)
@@ -591,9 +602,9 @@
         V((CP, 256), F32),
         DMA((6,)),
         DMA((12,)),
-        DMA((items, 12)),
+        DMA((items, 11)),
         DMA((14,)),
-        DMA((2 * experts, 14)),
+        DMA((items, 8)),
         DMA((2, 3)),
         DMA((2, 34)),
         DMA((2, 3)),

time: 130 us -> 128 us (0.985)
  Pallas kernels: 129 us -> 127 us
    pallas_call x1, Pallas kernels: 126 us -> 125 us  [body(): call(tokens.T, cotangent.T, routes.T, combine.T, w_gate, w_up, jnp.swapax...]
where the time goes in v4:
time: 128 us
  Pallas kernels  127 us (99%)
    pallas_call x1, Pallas kernels, body(): call(tokens.T, cotangent.T, routes.T, combine.T, w_gate, w_up, jnp.swapax...  125 us

profile of v4, /device:TPU:2, one launch (start us, length us, event | category | flops | bytes accessed | tf_op | source)
XLA Modules:
  0.0 127.9 jit_solution(2895212253425172433)
XLA Ops:
  0.6 124.8 %shard_map.110 = (bf16[224,128]{1,0:T(8,128)(2,1)S(1)}, bf16[224,128]{1,0:T(8,128)(2,1)S(1)}, bf16[3,3,224,1280]{3,2,1,0:T(8,128)(2,1)S(1)}) custom-call(bf16[224,128]{1,0:T(8,128)(2,1)} %bitcast.11, bf16[224,128]{1,0:T(8,128)(2,1)} %bitcast.12, s32[8,2048]{1,0:T(8,128)} %bitcast.9, f32[8,2048]{1,0:T(8,128)} %bitcast.10, bf16[3,224,1280]{2,1,0:T(8,128)(2,1)} %wg.1, ...), custom_call_target="tpu_custom_call" | custom-call | tf_op jit(solution)/shard_map/pallas_call | solution.py:625
  125.4 2.5 %shard_map.111 = (bf16[224,128]{1,0:T(8,128)(2,1)}, bf16[224,128]{1,0:T(8,128)(2,1)}, bf16[3,224,1280]{2,1,0:T(8,128)(2,1)}, bf16[3,224,1280]{2,1,0:T(8,128)(2,1)}, bf16[3,224,1280]{2,1,0:T(8,128)(2,1)}) custom-call(bf16[224,128]{1,0:T(8,128)(2,1)S(1)} %get-tuple-element.13.mixed, bf16[224,128]{1,0:T(8,128)(2,1)S(1)} %get-tuple-element.14.grad_tokens, ...), custom_call_target="tpu_custom_call" | custom-call | tf_op jit(solution)/shard_map/pallas_call | solution.py:628

commit v5 on v4

--- a/solution.py
+++ b/solution.py
@@ -9,7 +9,7 @@
 BF = jnp.bfloat16
 F32 = jnp.float32
 
-SUM_AT = (0, 1, 2, 3, 4)
+SUM_AT = (0, 2, 3, 4, 5)
 GATHER_AT = (0, 1, 2, 3, 4)
 CP = 384
 ROWS = 48

time: 128 us -> 131 us (1.023)
  Pallas kernels: 127 us -> 130 us
    pallas_call x1, Pallas kernels: 125 us -> 128 us  [body(): call(tokens.T, cotangent.T, routes.T, combine.T, w_gate, w_up, jnp.swapax...]
where the time goes in v5:
time: 131 us
  Pallas kernels  130 us (99%)
    pallas_call x1, Pallas kernels, body(): call(tokens.T, cotangent.T, routes.T, combine.T, w_gate, w_up, jnp.swapax...  128 us

profile of v5, /device:TPU:2, one launch (start us, length us, event | category | flops | bytes accessed | tf_op | source)
XLA Modules:
  0.0 130.8 jit_solution(4485957659857371749)
XLA Ops:
  0.6 127.6 %shard_map.110 = (bf16[224,128]{1,0:T(8,128)(2,1)S(1)}, bf16[224,128]{1,0:T(8,128)(2,1)S(1)}, bf16[3,3,224,1280]{3,2,1,0:T(8,128)(2,1)S(1)}) custom-call(bf16[224,128]{1,0:T(8,128)(2,1)} %bitcast.11, bf16[224,128]{1,0:T(8,128)(2,1)} %bitcast.12, s32[8,2048]{1,0:T(8,128)} %bitcast.9, f32[8,2048]{1,0:T(8,128)} %bitcast.10, bf16[3,224,1280]{2,1,0:T(8,128)(2,1)} %wg.1, ...), custom_call_target="tpu_custom_call" | custom-call | tf_op jit(solution)/shard_map/pallas_call | solution.py:625
  128.3 2.5 %shard_map.111 = (bf16[224,128]{1,0:T(8,128)(2,1)}, bf16[224,128]{1,0:T(8,128)(2,1)}, bf16[3,224,1280]{2,1,0:T(8,128)(2,1)}, bf16[3,224,1280]{2,1,0:T(8,128)(2,1)}, bf16[3,224,1280]{2,1,0:T(8,128)(2,1)}) custom-call(bf16[224,128]{1,0:T(8,128)(2,1)S(1)} %get-tuple-element.13.mixed, bf16[224,128]{1,0:T(8,128)(2,1)S(1)} %get-tuple-element.14.grad_tokens, ...), custom_call_target="tpu_custom_call" | custom-call | tf_op jit(solution)/shard_map/pallas_call | solution.py:628
